TPU v7x, 512 devices: a whole 4x4x16 slice. The times are simulated.
512 devices in a mesh: cd: 128 (over x, z, core), ij: 4 (over y).
Axes of the slice: x: 4, y: 4, z: 16, core: 2. Of those that a mesh axis runs over, the one named last changes fastest.
Arguments:
- amplitudes: bfloat16 [4, 512, 32768], P('ij', 'cd'), may hold values from -6 to 6
- integrals: bfloat16 [1152, 32768], P(None, 'cd'), may hold values from -0.25 to 0.25
- pair_irrep: int32 [4, 512], P('ij'), may hold values from 0 to 7
- cd_irrep: int32 [32768], P('cd'), may hold values from 0 to 7
- ab_irrep: int32 [1152], P('cd'), may hold values from 0 to 7
Outputs:
- ladder: bfloat16 [4, 512, 1152], P('ij', None, 'cd')
All inputs are finite; a program needn't handle non-finite values.
Results may differ from a plain program's by a relative error of at most 0.0035.
Values may be sent and summed in bfloat16 or wider, within the bound.
No kernel may reach another device: no remote copies, remote signals or barrier semaphores. Data moves between devices by JAX's collectives and lax.ppermute only.
A program may use at most 64 MiB of HBM per device.

v0:
```python
import jax
import jax.numpy as jnp
from jax import lax
from jax.sharding import PartitionSpec as P


def body(amplitudes, integrals, pair_irrep, cd_irrep, ab_irrep):
    relaid = lax.all_to_all(amplitudes, "cd", split_axis=2, concat_axis=1, tiled=True)[0]
    row_labels = pair_irrep[0]
    symmetric = jnp.where(row_labels[:, None] == cd_irrep[None, :], relaid, jnp.zeros_like(relaid))
    partial_value = lax.dot_general(
        symmetric, integrals, (((1,), (1,)), ((), ())), preferred_element_type=jnp.float32
    )
    summed = lax.psum_scatter(partial_value, "cd", scatter_dimension=1, tiled=True)
    result = jnp.where(row_labels[:, None] == ab_irrep[None, :], summed, jnp.zeros_like(summed))
    return result.astype(jnp.bfloat16)[None]


def solution(mesh):
    placed = (P("ij", "cd", None), P(None, "cd"), P("ij", None), P("cd"), P("cd"))
    return jax.shard_map(
        body, mesh=mesh, in_specs=placed, out_specs=P("ij", None, "cd"), check_vma=False
    )
```

profile of v0, /device:TPU:24, one launch (start us, length us, event | category | flops | bytes accessed | tf_op | source)
XLA Modules:
  0.0 851.4 jit_solution(6383370314222650321)
XLA Ops:
  0.0 0.0 copy-start
  0.0 29.8 %copy.9 = bf16[1,4,32768]{1,0,2:T(2,128)(2,1)} copy(bf16[1,4,32768]{2,1,0:T(4,128)(2,1)} %param.5) | data formatting | bytes 524288 | tf_op args[0]
  29.8 0.5 broadcast.2
  30.3 179.1 %reduce = bf16[32768,4]{1,0:T(8,128)(2,1)} reduce(bf16[32768,1,4]{2,1,0:T(2,128)(2,1)} %bitcast.16, bf16[]{:T(256)} %broadcast.2), dimensions={1}, to_apply=%bitcast.11.reduce_sub_computation | reduce | bytes 524290
  209.5 16.8 %reshape.5 = bf16[128,2,512]{2,1,0:T(2,128)(2,1)} reshape(bf16[32768,4]{1,0:T(8,128)(2,1)} %reduce) | data formatting | bytes 524288
  226.3 19.8 %all-to-all-start = ((bf16[128,2,512]{2,1,0:T(2,128)(2,1)}), bf16[128,2,512]{2,1,0:T(2,128)(2,1)S(1)}, u32[]{:S(2)}, u32[]{:S(2)}) async-start(bf16[128,2,512]{2,1,0:T(2,128)(2,1)} %reshape.5), calls=%async_computation | async-start | bytes 524288 | tf_op jit(solution)/shard_map/all_to_all | solution.py:8
  246.1 1.3 dynamic-slice
  248.0 21.8 %all-to-all-done = bf16[128,2,512]{2,1,0:T(2,128)(2,1)S(1)} async-done(((bf16[128,2,512]{2,1,0:T(2,128)(2,1)}), bf16[128,2,512]{2,1,0:T(2,128)(2,1)S(1)}, u32[]{:S(2)}, u32[]{:S(2)}) %all-to-all-start) | async-done | bytes 262176 | tf_op jit(solution)/shard_map/all_to_all | solution.py:8
  269.8 34.0 %reshape.6 = bf16[32768,1,4]{2,1,0:T(2,128)(2,1)} reshape(bf16[128,2,512]{2,1,0:T(2,128)(2,1)S(1)} %all-to-all-done) | data formatting | bytes 524288
  303.8 0.0 copy-start.1
  303.8 0.0 copy-start.2
  303.8 30.6 %copy.10 = bf16[1,4,32768]{2,1,0:T(4,128)(2,1)S(1)} copy(bf16[1,4,32768]{1,0,2:T(2,128)(2,1)} %bitcast.17) | data formatting | bytes 524288 | tf_op jit(solution)/shard_map/all_to_all | solution.py:8
  334.4 0.2 copy.11
  334.6 0.1 squeeze.3
  334.7 0.0 copy-done
  334.7 0.0 copy-done.1
  334.7 0.0 copy-done.2
  334.7 0.6 fusion
  335.3 0.0 copy-start.3
  335.3 514.7 %all-reduce.2 = bf16[512,1152]{0,1:T(8,128)(2,1)} all-reduce(f32[512,1152]{0,1:T(8,128)S(1)} %fusion), channel_id=2, replica_groups=mesh['cd'=128,'ij'=4] {'cd'}, use_global_device_ids=true, to_apply=%region_0.1.clone | all-reduce | flops 589824 | bytes 3538944
  850.0 0.0 copy-done.3
  850.0 1.4 fusion.5
  (1 shorter events, 0.0 us)
Async XLA Ops:
  0.0 334.7 %copy-start = (bf16[1152,256]{1,0:T(8,128)(2,1)S(1)}, bf16[1152,256]{1,0:T(8,128)(2,1)}, u32[]{:S(2)}) copy-start(bf16[1152,256]{1,0:T(8,128)(2,1)} %param.6) | copy-start | bytes 1769476
  226.3 43.5 %all-to-all-start = ((bf16[128,2,512]{2,1,0:T(2,128)(2,1)}), bf16[128,2,512]{2,1,0:T(2,128)(2,1)S(1)}, u32[]{:S(2)}, u32[]{:S(2)}) async-start(bf16[128,2,512]{2,1,0:T(2,128)(2,1)} %reshape.5), calls=%async_computation | async-start | bytes 524288 | tf_op jit(solution)/shard_map/all_to_all | solution.py:8
  303.8 31.0 %copy-start.1 = (s32[1,512]{1,0:T(1,128)S(1)}, s32[1,512]{1,0:T(1,128)}, u32[]{:S(2)}) copy-start(s32[1,512]{1,0:T(1,128)} %param.7) | copy-start | bytes 6148
  303.8 31.0 %copy-start.2 = (s32[256]{0:T(256)S(1)}, s32[256]{0:T(256)}, u32[]{:S(2)}) copy-start(s32[256]{0:T(256)} %param.8) | copy-start | bytes 3076
  335.3 514.7 %copy-start.3 = (s32[9]{0:T(128)S(1)}, s32[9]{0:T(128)}, u32[]{:S(2)}) copy-start(s32[9]{0:T(128)} %param.9) | copy-start | bytes 112
where the time goes:
time: 854 us; the launch traced here: 851 us
  blocking collectives  515 us (60%)
  other arithmetic  181 us (21%)
  local copies, waits for them, and re-layouts  113 us (13%)
  waiting for transfers between devices  21.8 us (3%)
  starting transfers between devices  19.8 us (2%)
    unnamed x1, blocking collectives  515 us
    unnamed x1, other arithmetic  179 us
    unnamed x14, local copies, waits for them, and re-layouts  82.4 us
    all_to_all x2, local copies, waits for them, and re-layouts, body(): lax.all_to_all(amplitudes, 'cd', split_axis=2, concat_axis=1, tiled=True)[0]  30.8 us
    all_to_all x1, waiting for transfers between devices, body(): lax.all_to_all(amplitudes, 'cd', split_axis=2, concat_axis=1, tiled=True)[0]  21.8 us
    all_to_all x1, starting transfers between devices, body(): lax.all_to_all(amplitudes, 'cd', split_axis=2, concat_axis=1, tiled=True)[0]  19.8 us
  transfers between devices with their start and end apart: 1, of which 1 were waited for; matrix products, arithmetic and copies ran while one was open for 0% of the time, Pallas kernels for 0%

commit v1 on v0

v1 whole, which is shorter than its diff:
```python
import jax
import jax.numpy as jnp
from jax import lax
from jax.experimental import pallas as pl
from jax.experimental.pallas import tpu as pltpu
from jax.sharding import Mesh, PartitionSpec as P

X, Z, CORES, Y = 4, 16, 2, 4
ROWS = 4
OWN = 9
CDS = 256
AB = X * Z * CORES * OWN
LABELLED = AB + 16
CUT = 576
GROUP = Z * CORES * ROWS
BF, F32 = jnp.bfloat16, jnp.float32
VMEM = pl.BlockSpec(memory_space=pltpu.VMEM)


def prepare_kernel(amps, integrals, labels, sent, labelled):
    for x in range(X):
        for zc in range(Z * CORES):
            start = (x * Z * CORES + zc) * CDS
            sent[zc, :, x * CDS:(x + 1) * CDS] = amps[0, :, start:start + CDS]
    labelled[:AB] = integrals[...]
    row = labels[...].astype(F32)
    labelled[AB:] = jnp.broadcast_to(row, (16, CDS)).astype(BF)


def multiply_kernel(place, amps, rows, own, left, right, far_top, far_bottom, mine, other, stacked, acc):
    x, core = place[0], place[1]
    for zc in range(Z * CORES):
        block = amps[zc].astype(F32)
        for k in range(X):
            stacked[k, zc * ROWS:(zc + 1) * ROWS, :] = block[:, k * CDS:(k + 1) * CDS]
    row_labels = rows[...]

    def masked(k, labels):
        values = stacked[k]
        labels = labels.astype(F32)[:1]
        return jnp.where(row_labels == labels, values, jnp.zeros_like(values)).astype(BF)

    def times(block, values):
        return lax.dot_general(block, values, (((1,), (1,)), ((), ())), preferred_element_type=F32)

    a_own = masked(x, own[AB:])
    a_left = masked(lax.rem(x + X - 1, X), left[AB:])
    a_right = masked(lax.rem(x + 1, X), right[AB:])
    a_far = masked(lax.rem(x + 2, X), far_bottom[AB - CUT:])
    step = 192
    for start in range(0, AB, step):
        part = pl.ds(start, step)
        far = far_top[part] if start < CUT else far_bottom[pl.ds(start - CUT, step)]
        acc[part] = (times(own[part], a_own) + times(left[part], a_left)) + (
            times(right[part], a_right) + times(far, a_far))
    first = core == 0
    for z in range(Z):
        for k in range(X):
            start = (k * Z + z) * CORES * OWN
            low, high = acc[start:start + OWN], acc[start + OWN:start + 2 * OWN]
            mine[z, k * OWN:(k + 1) * OWN, :] = jnp.where(first, low, high)
            other[z, k * OWN:(k + 1) * OWN, :] = jnp.where(first, high, low)


def sum_kernel(partials, out, total):
    value = partials[0].astype(F32)
    for z in range(1, Z):
        value = value + partials[z].astype(F32)
    total[...] = value
    for k in range(X):
        out[k] = total[k * OWN:(k + 1) * OWN, :].astype(BF)


def finish_kernel(parts, rows, abs_, out):
    for k in range(X):
        lanes = slice(k * GROUP, (k + 1) * GROUP)
        value = parts[k].astype(F32)
        keep = rows[:, lanes] == abs_[...]
        out[:, lanes] = jnp.where(keep, value, jnp.zeros_like(value)).astype(BF)


def call(kernel, out_shape, scratch=(), specs=None, n=0):
    return pl.pallas_call(
        kernel,
        out_shape=out_shape,
        in_specs=[pl.BlockSpec(memory_space=pltpu.SMEM)] * n + [VMEM] * (specs - n),
        out_specs=jax.tree.map(lambda _: VMEM, out_shape),
        scratch_shapes=list(scratch),
        compiler_params=pltpu.CompilerParams(vmem_limit_bytes=40 * 2**20),
    )


def body(amplitudes, integrals, pair_irrep, cd_irrep, ab_irrep):
    shape = jax.ShapeDtypeStruct
    x, core = lax.axis_index("x"), lax.axis_index("core")
    sent, labelled = call(
        prepare_kernel,
        (shape((Z * CORES, ROWS, X * CDS), BF), shape((LABELLED, CDS), BF)),
        specs=3,
    )(amplitudes, integrals, cd_irrep[None])
    up = [(i, (i + 1) % X) for i in range(X)]
    down = [(i, (i - 1) % X) for i in range(X)]
    left = lax.ppermute(labelled, "x", up)
    right = lax.ppermute(labelled, "x", down)
    amps = lax.all_to_all(sent, ("z", "core"), 0, 0, tiled=True)
    far_top = lax.ppermute(left[:CUT], "x", up)
    far_bottom = lax.ppermute(right[CUT:], "x", down)
    rows = lax.dynamic_slice_in_dim(pair_irrep.reshape(X, GROUP), x, 1, 0)
    rows = rows.reshape(GROUP, 1).astype(F32)
    place = jnp.stack([x, core]).astype(jnp.int32)
    sums = shape((Z, X * OWN, GROUP), F32)
    mine, other = call(
        multiply_kernel,
        (sums, sums),
        scratch=[pltpu.VMEM((X, GROUP, CDS), F32), pltpu.VMEM((AB, GROUP), F32)],
        specs=8, n=1,
    )(place, amps, rows, labelled, left, right, far_top, far_bottom)
    theirs = lax.ppermute(other, "core", [(0, 1), (1, 0)])
    partials = (mine + theirs).astype(BF)
    partials = lax.all_to_all(partials, "z", 0, 0, tiled=True)
    parts = call(
        sum_kernel, shape((X, OWN, GROUP), BF), scratch=[pltpu.VMEM((X * OWN, GROUP), F32)], specs=1
    )(partials)
    parts = lax.all_to_all(parts, "x", 0, 0, tiled=True)
    out = call(finish_kernel, shape((OWN, X * GROUP), BF), specs=3)(parts, pair_irrep, ab_irrep[:, None])
    return out.T[None]


def solution(mesh):
    split = Mesh(mesh.devices.reshape(X, Z, CORES, Y), ("x", "z", "core", "y"))
    cd = ("x", "z", "core")
    placed = (P("y", cd, None), P(None, cd), P("y", None), P(cd), P(cd))
    return jax.shard_map(body, mesh=split, in_specs=placed, out_specs=P("y", None, cd), check_vma=False)
```

time: 854 us -> 95.9 us (0.11)
  blocking collectives: 515 us -> 26.7 us
  other arithmetic: 181 us -> 0.12 us
  local copies, waits for them, and re-layouts: 113 us -> 4.27 us
  starting transfers between devices: 19.8 us -> 34.8 us
    unnamed x1 -> x0, blocking collectives: 515 us -> none
    unnamed x1 -> x0, other arithmetic: 179 us -> none
    unnamed x14 -> x10, local copies, waits for them, and re-layouts: 82.4 us -> 4.02 us
    all_to_all x2 -> x0, local copies, waits for them, and re-layouts: 30.8 us -> none  [body(): lax.all_to_all(amplitudes, 'cd', split_axis=2, concat_axis=1, tiled=True)[0]]
    all_to_all x0 -> x1, blocking collectives: none -> 26.7 us  [body(): partials = lax.all_to_all(partials, 'z', 0, 0, tiled=True)]
    ppermute x0 -> x5, waiting for transfers between devices: none -> 21.2 us  [the longest x1 11.3 us: body(): right = lax.ppermute(labelled, 'x', down)]
    all_to_all x1 -> x2, waiting for transfers between devices: 21.8 us -> 4.58 us  [the longest x1 4.57 us: body(): parts = lax.all_to_all(parts, 'x', 0, 0, tiled=True)]
    ppermute x0 -> x5, starting transfers between devices: none -> 16 us  [the longest x1 5.6 us: body(): far_bottom = lax.ppermute(right[CUT:], 'x', down)]
  transfers between devices with their start and end apart: 1 -> 7, of which waited for: 1 -> 4; matrix products, arithmetic and copies ran while one was open for 0% -> 0% of each run, Pallas kernels for 0% -> 0%
where the time goes in v1:
time: 95.9 us; the launch traced here: 95.4 us
  starting transfers between devices  34.8 us (36%)
  blocking collectives  26.7 us (28%)
  waiting for transfers between devices  25.8 us (27%)
  local copies, waits for them, and re-layouts  4.27 us (4%)
  Pallas kernels  3.56 us (4%)
    all_to_all x1, blocking collectives, body(): partials = lax.all_to_all(partials, 'z', 0, 0, tiled=True)  26.7 us
    all_to_all x1, starting transfers between devices, body(): amps = lax.all_to_all(sent, ('z', 'core'), 0, 0, tiled=True)  15.5 us
    ppermute x1, waiting for transfers between devices, body(): right = lax.ppermute(labelled, 'x', down)  11.3 us
    ppermute x1, waiting for transfers between devices, body(): far_top = lax.ppermute(left[:CUT], 'x', up)  8.38 us
    ppermute x1, starting transfers between devices, body(): far_bottom = lax.ppermute(right[CUT:], 'x', down)  5.6 us
    ppermute x1, starting transfers between devices, body(): right = lax.ppermute(labelled, 'x', down)  4.67 us
    all_to_all x1, waiting for transfers between devices, body(): parts = lax.all_to_all(parts, 'x', 0, 0, tiled=True)  4.57 us
    unnamed x10, local copies, waits for them, and re-layouts  4.02 us
  transfers between devices with their start and end apart: 7, of which 4 were waited for; matrix products, arithmetic and copies ran while one was open for 0% of the time, Pallas kernels for 0%

profile of v1, /device:TPU:24, one launch (start us, length us, event | category | flops | bytes accessed | tf_op | source)
XLA Modules:
  0.0 95.4 jit_solution(1829869959558542285)
XLA Ops:
  0.0 0.0 copy-start.3
  0.0 0.7 copy-done.3
  0.7 0.0 copy-start
  0.7 1.1 %copy-done = bf16[1152,256]{1,0:T(8,128)(2,1)S(1)} copy-done((bf16[1152,256]{1,0:T(8,128)(2,1)S(1)}, bf16[1152,256]{1,0:T(8,128)(2,1)}, u32[]{:S(2)}) %copy-start) | copy-done | bytes 589848
  1.7 0.0 copy-start.1
  1.7 0.9 copy-done.1
  2.7 0.8 shard_map.55
  3.5 15.5 %all-to-all-start = ((bf16[32,4,1024]{2,1,0:T(4,128)(2,1)}), bf16[32,4,1024]{2,1,0:T(4,128)(2,1)S(1)}, u32[]{:S(2)}, u32[]{:S(2)}) async-start(bf16[32,4,1024]{2,1,0:T(4,128)(2,1)} %get-tuple-element.9), calls=%async_computation | async-start | bytes 524288 | tf_op jit(solution)/shard_map/all_to_all | solution.py:105
  19.0 4.7 %collective-permute-start.1 = (bf16[1168,256]{1,0:T(8,128)(2,1)S(1)}, bf16[1168,256]{1,0:T(8,128)(2,1)S(1)}, u32[]{:S(2)}, u32[]{:S(2)}) collective-permute-start(bf16[1168,256]{1,0:T(8,128)(2,1)S(1)} %get-tuple-element.10.own), channel_id=1, source_target_pairs={{0,384},{128,0},{256,128},{384,256},{1,385},{129,1},{257,129},{385... | collective-permute-start | bytes 1794056 | tf_op jit(solution)/shard_map/ppermute | solution.py:104
  23.6 1.9 %collective-permute-start = (bf16[1168,256]{1,0:T(8,128)(2,1)S(1)}, bf16[1168,256]{1,0:T(8,128)(2,1)S(1)}, u32[]{:S(2)}, u32[]{:S(2)}) collective-permute-start(bf16[1168,256]{1,0:T(8,128)(2,1)S(1)} %get-tuple-element.10.own), channel_id=1, source_target_pairs={{0,128},{128,256},{256,384},{384,0},{1,129},{129,257},{257,385},{3... | collective-permute-start | bytes 1794056 | tf_op jit(solution)/shard_map/ppermute | solution.py:103
  25.6 11.3 %collective-permute-done.1.right = bf16[1168,256]{1,0:T(8,128)(2,1)S(1)} collective-permute-done((bf16[1168,256]{1,0:T(8,128)(2,1)S(1)}, bf16[1168,256]{1,0:T(8,128)(2,1)S(1)}, u32[]{:S(2)}, u32[]{:S(2)}) %collective-permute-start.1) | collective-permute-done | bytes 598048 | tf_op jit(solution)/shard_map/ppermute | solution.py:104
  36.8 5.6 %collective-permute-start.3 = (bf16[592,256]{1,0:T(8,128)(2,1)S(1)}, bf16[592,256]{1,0:T(8,128)(2,1)S(1)}, u32[]{:S(2)}, u32[]{:S(2)}) collective-permute-start(bf16[592,256]{1,0:T(8,128)(2,1)S(1)} %slice.9), channel_id=1, source_target_pairs={{0,384},{128,0},{256,128},{384,256},{1,385},{129,1},{257,129},{385... | collective-permute-start | bytes 909320 | tf_op jit(solution)/shard_map/ppermute | solution.py:107
  42.5 0.0 collective-permute-done.left
  42.5 1.9 %collective-permute-start.2 = (bf16[576,256]{1,0:T(8,128)(2,1)S(1)}, bf16[576,256]{1,0:T(8,128)(2,1)S(1)}, u32[]{:S(2)}, u32[]{:S(2)}) collective-permute-start(bf16[576,256]{1,0:T(8,128)(2,1)S(1)} %slice.8), channel_id=1, source_target_pairs={{0,128},{128,256},{256,384},{384,0},{1,129},{129,257},{257,385},{3... | collective-permute-start | bytes 884744 | tf_op jit(solution)/shard_map/ppermute | solution.py:106
  44.4 0.0 copy-start.2
  44.4 0.7 copy-done.2
  45.1 0.1 copy.6.rows
  45.2 0.1 pad_add_fusion.place
  45.3 8.4 %collective-permute-done.2.far_top = bf16[576,256]{1,0:T(8,128)(2,1)S(1)} collective-permute-done((bf16[576,256]{1,0:T(8,128)(2,1)S(1)}, bf16[576,256]{1,0:T(8,128)(2,1)S(1)}, u32[]{:S(2)}, u32[]{:S(2)}) %collective-permute-start.2) | collective-permute-done | bytes 294944 | tf_op jit(solution)/shard_map/ppermute | solution.py:106
  53.7 0.0 collective-permute-done.3.far_bottom
  53.7 0.0 all-to-all-done.amps
  53.7 1.5 %shard_map.56 = (f32[16,36,128]{2,1,0:T(8,128)S(1)}, f32[16,36,128]{2,1,0:T(8,128)S(1)}) custom-call(s32[2]{0:T(128)S(1)} %pad_add_fusion.place, bf16[32,4,1024]{2,1,0:T(4,128)(2,1)S(1)} %all-to-all-done.amps, f32[128,1]{1,0:T(8,128)S(1)} %copy.6.rows, bf16[1168,256]{1,0:T(8,128)(2,1)S(1)} %get-tuple-element.10.own, ...), custom_call_target="tpu_custom_call" | custom-call | tf_op jit(solution)/shard_map/pallas_call | solution.py:112
  55.2 1.9 %collective-permute-start.4 = (f32[16,36,128]{2,1,0:T(8,128)S(1)}, f32[16,36,128]{2,1,0:T(8,128)S(1)}, u32[]{:S(2)}, u32[]{:S(2)}) collective-permute-start(f32[16,36,128]{2,1,0:T(8,128)S(1)} %get-tuple-element.12), channel_id=1, source_target_pairs={{0,4},{4,0},{1,5},{5,1},{2,6},{6,2},{3,7},{7,3},{8,12},{12,8},{9,1... | collective-permute-start | bytes 884744 | tf_op jit(solution)/shard_map/ppermute | solution.py:118
  57.1 1.6 %collective-permute-done.4 = f32[16,36,128]{2,1,0:T(8,128)S(1)} collective-permute-done((f32[16,36,128]{2,1,0:T(8,128)S(1)}, f32[16,36,128]{2,1,0:T(8,128)S(1)}, u32[]{:S(2)}, u32[]{:S(2)}) %collective-permute-start.4) | collective-permute-done | bytes 294944 | tf_op jit(solution)/shard_map/ppermute | solution.py:118
  58.7 26.7 %all_to_all.15.partials = bf16[16,36,128]{2,1,0:T(8,128)(2,1)S(1)} all-to-all(bf16[16,36,128]{2,1,0:T(8,128)(2,1)S(1)} %add_convert_fusion), channel_id=1, replica_groups=mesh['x'=4,'z'=16,'core'=2,'y'=4] {'z'}, dimensions={0} | all-to-all | bytes 294912 | tf_op jit(solution)/shard_map/all_to_all | solution.py:120
  85.5 0.6 shard_map.57
  86.1 3.3 %all-to-all-start.2 = ((bf16[4,9,128]{2,1,0:T(8,128)(2,1)}), bf16[4,9,128]{2,1,0:T(8,128)(2,1)S(1)}, u32[]{:S(2)}, u32[]{:S(2)}) async-start(bf16[4,9,128]{2,1,0:T(8,128)(2,1)} %shard_map.57), calls=%async_computation.2 | async-start | bytes 32768 | tf_op jit(solution)/shard_map/all_to_all | solution.py:124
  89.4 0.0 copy-start.4
  89.4 0.6 copy-done.4
  90.0 0.1 copy.7.abs_
  90.1 4.6 %all-to-all-done.2.parts = bf16[4,9,128]{2,1,0:T(8,128)(2,1)S(1)} async-done(((bf16[4,9,128]{2,1,0:T(8,128)(2,1)}), bf16[4,9,128]{2,1,0:T(8,128)(2,1)S(1)}, u32[]{:S(2)}, u32[]{:S(2)}) %all-to-all-start.2) | async-done | bytes 9248 | tf_op jit(solution)/shard_map/all_to_all | solution.py:124
  94.7 0.7 shard_map.58
  (4 shorter events, 0.1 us)
Async XLA Ops:
  0.0 0.7 copy-start.3
  0.7 1.1 %copy-start = (bf16[1152,256]{1,0:T(8,128)(2,1)S(1)}, bf16[1152,256]{1,0:T(8,128)(2,1)}, u32[]{:S(2)}) copy-start(bf16[1152,256]{1,0:T(8,128)(2,1)} %integrals.1) | copy-start | bytes 1769476
  1.7 0.9 copy-start.1
  3.5 50.2 %all-to-all-start = ((bf16[32,4,1024]{2,1,0:T(4,128)(2,1)}), bf16[32,4,1024]{2,1,0:T(4,128)(2,1)S(1)}, u32[]{:S(2)}, u32[]{:S(2)}) async-start(bf16[32,4,1024]{2,1,0:T(4,128)(2,1)} %get-tuple-element.9), calls=%async_computation | async-start | bytes 524288 | tf_op jit(solution)/shard_map/all_to_all | solution.py:105
  19.0 17.9 %collective-permute-start.1 = (bf16[1168,256]{1,0:T(8,128)(2,1)S(1)}, bf16[1168,256]{1,0:T(8,128)(2,1)S(1)}, u32[]{:S(2)}, u32[]{:S(2)}) collective-permute-start(bf16[1168,256]{1,0:T(8,128)(2,1)S(1)} %get-tuple-element.10.own), channel_id=1, source_target_pairs={{0,384},{128,0},{256,128},{384,256},{1,385},{129,1},{257,129},{385... | collective-permute-start | bytes 1794056 | tf_op jit(solution)/shard_map/ppermute | solution.py:104
  23.6 18.8 %collective-permute-start = (bf16[1168,256]{1,0:T(8,128)(2,1)S(1)}, bf16[1168,256]{1,0:T(8,128)(2,1)S(1)}, u32[]{:S(2)}, u32[]{:S(2)}) collective-permute-start(bf16[1168,256]{1,0:T(8,128)(2,1)S(1)} %get-tuple-element.10.own), channel_id=1, source_target_pairs={{0,128},{128,256},{256,384},{384,0},{1,129},{129,257},{257,385},{3... | collective-permute-start | bytes 1794056 | tf_op jit(solution)/shard_map/ppermute | solution.py:103
  36.8 16.9 %collective-permute-start.3 = (bf16[592,256]{1,0:T(8,128)(2,1)S(1)}, bf16[592,256]{1,0:T(8,128)(2,1)S(1)}, u32[]{:S(2)}, u32[]{:S(2)}) collective-permute-start(bf16[592,256]{1,0:T(8,128)(2,1)S(1)} %slice.9), channel_id=1, source_target_pairs={{0,384},{128,0},{256,128},{384,256},{1,385},{129,1},{257,129},{385... | collective-permute-start | bytes 909320 | tf_op jit(solution)/shard_map/ppermute | solution.py:107
  42.5 11.2 %collective-permute-start.2 = (bf16[576,256]{1,0:T(8,128)(2,1)S(1)}, bf16[576,256]{1,0:T(8,128)(2,1)S(1)}, u32[]{:S(2)}, u32[]{:S(2)}) collective-permute-start(bf16[576,256]{1,0:T(8,128)(2,1)S(1)} %slice.8), channel_id=1, source_target_pairs={{0,128},{128,256},{256,384},{384,0},{1,129},{129,257},{257,385},{3... | collective-permute-start | bytes 884744 | tf_op jit(solution)/shard_map/ppermute | solution.py:106
  44.4 0.7 copy-start.2
  55.2 3.5 %collective-permute-start.4 = (f32[16,36,128]{2,1,0:T(8,128)S(1)}, f32[16,36,128]{2,1,0:T(8,128)S(1)}, u32[]{:S(2)}, u32[]{:S(2)}) collective-permute-start(f32[16,36,128]{2,1,0:T(8,128)S(1)} %get-tuple-element.12), channel_id=1, source_target_pairs={{0,4},{4,0},{1,5},{5,1},{2,6},{6,2},{3,7},{7,3},{8,12},{12,8},{9,1... | collective-permute-start | bytes 884744 | tf_op jit(solution)/shard_map/ppermute | solution.py:118
  86.1 8.6 %all-to-all-start.2 = ((bf16[4,9,128]{2,1,0:T(8,128)(2,1)}), bf16[4,9,128]{2,1,0:T(8,128)(2,1)S(1)}, u32[]{:S(2)}, u32[]{:S(2)}) async-start(bf16[4,9,128]{2,1,0:T(8,128)(2,1)} %shard_map.57), calls=%async_computation.2 | async-start | bytes 32768 | tf_op jit(solution)/shard_map/all_to_all | solution.py:124
  89.4 0.7 copy-start.4

commit v2 on v0

v2 whole, which is shorter than its diff:
```python
import jax
import jax.numpy as jnp
from jax import lax
from jax.experimental import pallas as pl
from jax.experimental.pallas import tpu as pltpu
from jax.sharding import Mesh, PartitionSpec as P

X, Z, CORES, Y = 4, 16, 2, 4
ROWS = 4
OWN = 9
CDS = 256
PART = Z * CORES * OWN
TALL = PART + 16
WIDE = CORES * CDS
LINE = Z * ROWS
BF, F32 = jnp.bfloat16, jnp.float32
HBM = pl.BlockSpec(memory_space=pltpu.HBM)
VMEM = pl.BlockSpec(memory_space=pltpu.VMEM)
SMEM = pl.BlockSpec(memory_space=pltpu.SMEM)


def regroup_kernel(amps, sent, amps_in, sem):
    load = pltpu.make_async_copy(amps.at[0], amps_in, sem)
    load.start()
    load.wait()
    for x in range(X):
        for z in range(Z):
            start = (x * Z + z) * WIDE
            sent[z, :, x * WIDE:(x + 1) * WIDE] = amps_in[:, start:start + WIDE]


def slice_kernel(place, integrals, labels, *outs):
    row = jnp.broadcast_to(labels[...].astype(F32), (TALL - PART, CDS)).astype(BF)
    for step, out in enumerate(outs):
        start = lax.rem(place[0] + step, X) * PART
        out[:PART] = integrals[pl.ds(pl.multiple_of(start, 32), PART), :]
        out[PART:] = row


def stack_kernel(*refs):
    out = refs[-1]
    for step, ref in enumerate(refs[:-1]):
        out[step] = ref[...]


def multiply_kernel(place, *refs):
    amps, (rows, mine, other, out, stacked, acc) = refs[:X], refs[X:]
    x, first = place[0], place[1] == 0
    for step in range(X):
        source = lax.rem(x + X - step, X)
        for z in range(Z):
            stacked[source, z * ROWS:(z + 1) * ROWS, :] = amps[step][z].astype(F32)
    row_labels = rows[...]
    total = jnp.zeros((PART, X * LINE), F32)
    for step in range(X):
        source = lax.rem(x + X - step, X)
        lanes = pl.ds(pl.multiple_of(source * WIDE, WIDE), WIDE)
        values = jnp.concatenate([stacked[k, :, lanes] for k in range(X)], axis=0)
        halves = values[:, :CDS], values[:, CDS:]
        pairs = (
            (mine, jnp.where(first, halves[0], halves[1])),
            (other, jnp.where(first, halves[1], halves[0])),
        )
        for blocks, half in pairs:
            labels = blocks[step, PART:].astype(F32)[:1]
            kept = jnp.where(row_labels == labels, half, jnp.zeros_like(half)).astype(BF)
            total += lax.dot_general(
                blocks[step, :PART], kept, (((1,), (1,)), ((), ())), preferred_element_type=F32
            )
    acc[...] = total
    for z in range(Z):
        out[z] = acc[z * CORES * OWN:(z + 1) * CORES * OWN, :].astype(BF)


def sum_kernel(place, partials, own, sent, total):
    core = place[1]
    value = partials[0].astype(F32)
    for z in range(1, Z):
        value = value + partials[z].astype(F32)
    value = value.astype(BF)
    pairs = 2 * LINE
    i = lax.broadcasted_iota(jnp.int32, (pairs, CORES * pairs), 0)
    j = lax.broadcasted_iota(jnp.int32, (pairs, CORES * pairs), 1)
    goal = (i // ROWS) * (CORES * ROWS) + core * ROWS + lax.rem(i, ROWS)
    spread = jnp.where(j == goal, 1.0, 0.0).astype(BF)
    for k in range(X // 2):
        total[:, k * CORES * pairs:(k + 1) * CORES * pairs] = jnp.dot(
            value[:, k * pairs:(k + 1) * pairs], spread, preferred_element_type=F32
        )
    low, high = total[:OWN, :], total[OWN:, :]
    own[...] = jnp.where(core == 0, low, high).astype(BF)
    sent[...] = jnp.where(core == 0, high, low).astype(BF)


def finish_kernel(own, got, rows, abs_, out):
    value = own[...].astype(F32) + got[...].astype(F32)
    keep = rows[...] == abs_[...]
    out[...] = jnp.where(keep, value, jnp.zeros_like(value)).astype(BF)


def call(kernel, out_shape, in_specs, scratch=()):
    return pl.pallas_call(
        kernel,
        out_shape=out_shape,
        in_specs=in_specs,
        out_specs=jax.tree.map(lambda _: VMEM, out_shape),
        scratch_shapes=list(scratch),
        compiler_params=pltpu.CompilerParams(vmem_limit_bytes=32 * 2**20),
    )


def along_x(value, step):
    return lax.ppermute(value, "x", [(i, (i + step) % X) for i in range(X)])


def body(amplitudes, integrals, pair_irrep, cd_irrep, ab_irrep):
    shape = jax.ShapeDtypeStruct
    core = lax.axis_index("core")
    swap = [(0, 1), (1, 0)]
    place = jnp.stack([lax.axis_index("x"), core]).astype(jnp.int32)
    sent = call(
        regroup_kernel, shape((Z, ROWS, X * WIDE), BF), [HBM],
        [pltpu.VMEM((ROWS, X * Z * WIDE), BF), pltpu.SemaphoreType.DMA],
    )(amplitudes)
    amps = lax.all_to_all(sent, "z", 0, 0, tiled=True)
    slices = call(slice_kernel, (shape((TALL, CDS), BF),) * X, [SMEM, VMEM, VMEM])(place, integrals, cd_irrep[None])
    gathered = [slices[0]] + [along_x(slices[step], step) for step in range(1, X)]
    mine = call(stack_kernel, shape((X, TALL, CDS), BF), [VMEM] * X)(*gathered)
    other = lax.ppermute(mine, "core", swap)
    rows = lax.dynamic_slice_in_dim(pair_irrep.reshape(X * Z, CORES, ROWS), core, 1, 1)
    rows = rows.reshape(X * LINE, 1).astype(F32)
    all_amps = [amps] + [along_x(amps, step) for step in range(1, X)]
    partials = call(
        multiply_kernel, shape((Z, CORES * OWN, X * LINE), BF), [SMEM] + [VMEM] * (X + 3),
        [pltpu.VMEM((X, LINE, X * WIDE), F32), pltpu.VMEM((PART, X * LINE), F32)],
    )(place, *all_amps, rows, mine, other)
    partials = lax.all_to_all(partials, "z", 0, 0, tiled=True)
    final = shape((OWN, X * CORES * LINE), BF)
    own, away = call(
        sum_kernel, (final, final), [SMEM, VMEM], [pltpu.VMEM((CORES * OWN, X * CORES * LINE), F32)]
    )(place, partials)
    got = lax.ppermute(away, "core", swap)
    out = call(finish_kernel, final, [VMEM] * 4)(own, got, pair_irrep, ab_irrep[:, None])
    return out.T[None]


def solution(mesh):
    split = Mesh(mesh.devices.reshape(X, Z, CORES, Y), ("x", "z", "core", "y"))
    cd = ("x", "z", "core")
    placed = (P("y", cd, None), P(None, cd), P("y", None), P(cd), P(cd))
    return jax.shard_map(body, mesh=split, in_specs=placed, out_specs=P("y", None, cd), check_vma=False)
```

time: 854 us -> 90.9 us (0.11)
  blocking collectives: 515 us -> 27.9 us
  other arithmetic: 181 us -> 0.83 us
  local copies, waits for them, and re-layouts: 113 us -> 2.7 us
  starting transfers between devices: 19.8 us -> 41.6 us
  waiting for transfers between devices: 21.8 us -> 11.8 us
    unnamed x1 -> x0, blocking collectives: 515 us -> none
    unnamed x1, other arithmetic: 179 us -> 0.64 us
    unnamed x14 -> x11, local copies, waits for them, and re-layouts: 82.4 us -> 2.38 us
    all_to_all x2 -> x0, local copies, waits for them, and re-layouts: 30.8 us -> none  [body(): lax.all_to_all(amplitudes, 'cd', split_axis=2, concat_axis=1, tiled=True)[0]]
    all_to_all x0 -> x1, blocking collectives: none -> 27.9 us  [body(): partials = lax.all_to_all(partials, 'z', 0, 0, tiled=True)]
    ppermute x0 -> x8, starting transfers between devices: none -> 26.4 us  [the longest x6 22.6 us: along_x(): return lax.ppermute(value, 'x', [(i, (i + step) % X) for i in range(X)])]
    all_to_all x1, waiting for transfers between devices: 21.8 us -> 0.01 us  [body(): amps = lax.all_to_all(sent, 'z', 0, 0, tiled=True)]
    ppermute x0 -> x8, waiting for transfers between devices: none -> 11.8 us  [the longest x6 10.8 us: along_x(): return lax.ppermute(value, 'x', [(i, (i + step) % X) for i in range(X)])]
  transfers between devices with their start and end apart: 1 -> 9, of which waited for: 1 -> 5; matrix products, arithmetic and copies ran while one was open for 0% -> 2% of each run, Pallas kernels for 0% -> 1%
where the time goes in v2:
time: 90.9 us; the launch traced here: 89.3 us
  starting transfers between devices  41.6 us (46%)
  blocking collectives  27.9 us (31%)
  waiting for transfers between devices  11.8 us (13%)
  Pallas kernels  4.19 us (5%)
  local copies, waits for them, and re-layouts  2.7 us (3%)
    all_to_all x1, blocking collectives, body(): partials = lax.all_to_all(partials, 'z', 0, 0, tiled=True)  27.9 us
    ppermute x6, starting transfers between devices, along_x(): return lax.ppermute(value, 'x', [(i, (i + step) % X) for i in range(X)])  22.6 us
    all_to_all x1, starting transfers between devices, body(): amps = lax.all_to_all(sent, 'z', 0, 0, tiled=True)  15.2 us
    ppermute x6, waiting for transfers between devices, along_x(): return lax.ppermute(value, 'x', [(i, (i + step) % X) for i in range(X)])  10.8 us
    unnamed x11, local copies, waits for them, and re-layouts  2.38 us
    ppermute x1, starting transfers between devices, body(): other = lax.ppermute(mine, 'core', swap)  1.92 us
    ppermute x1, starting transfers between devices, body(): got = lax.ppermute(away, 'core', swap)  1.92 us
  transfers between devices with their start and end apart: 9, of which 5 were waited for; matrix products, arithmetic and copies ran while one was open for 2% of the time, Pallas kernels for 1%

profile of v2, /device:TPU:24, one launch (start us, length us, event | category | flops | bytes accessed | tf_op | source)
XLA Modules:
  0.0 89.3 jit_solution(12103586894023506731)
XLA Ops:
  0.0 0.0 copy-start
  0.0 0.0 copy-start.1
  0.0 1.0 %copy-done.1 = bf16[1,4,32768]{2,1,0:T(4,128)(2,1)S(1)} copy-done((bf16[1,4,32768]{2,1,0:T(4,128)(2,1)S(1)}, bf16[1,4,32768]{2,1,0:T(4,128)(2,1)}, u32[]{:S(2)}) %copy-start.1) | copy-done | bytes 262168
  1.0 0.8 shard_map.55
  1.8 15.2 %all-to-all-start = ((bf16[16,4,2048]{2,1,0:T(4,128)(2,1)}), bf16[16,4,2048]{2,1,0:T(4,128)(2,1)S(1)}, u32[]{:S(2)}, u32[]{:S(2)}) async-start(bf16[16,4,2048]{2,1,0:T(4,128)(2,1)} %shard_map.55), calls=%async_computation | async-start | bytes 524288 | tf_op jit(solution)/shard_map/all_to_all | solution.py:125
  17.0 0.1 pad_add_fusion.place
  17.1 0.0 copy-start.3
  17.1 0.0 copy-done
  17.1 0.7 copy-done.3
  17.8 0.6 shard_map.56
  18.4 3.4 %collective-permute-start.3 = (bf16[304,256]{1,0:T(8,128)(2,1)S(1)}, bf16[304,256]{1,0:T(8,128)(2,1)S(1)}, u32[]{:S(2)}, u32[]{:S(2)}) collective-permute-start(bf16[304,256]{1,0:T(8,128)(2,1)S(1)} %get-tuple-element.12), channel_id=1, source_target_pairs={{0,128},{128,256},{256,384},{384,0},{1,129},{129,257},{257,385},{3... | collective-permute-start | bytes 466952 | tf_op jit(solution)/shard_map/ppermute | solution.py:113
  21.8 4.6 %collective-permute-start.4 = (bf16[304,256]{1,0:T(8,128)(2,1)S(1)}, bf16[304,256]{1,0:T(8,128)(2,1)S(1)}, u32[]{:S(2)}, u32[]{:S(2)}) collective-permute-start(bf16[304,256]{1,0:T(8,128)(2,1)S(1)} %get-tuple-element.13), channel_id=1, source_target_pairs={{0,256},{128,384},{256,0},{384,128},{1,257},{129,385},{257,1},{385... | collective-permute-start | bytes 466952 | tf_op jit(solution)/shard_map/ppermute | solution.py:113
  26.4 3.3 %collective-permute-start.5 = (bf16[304,256]{1,0:T(8,128)(2,1)S(1)}, bf16[304,256]{1,0:T(8,128)(2,1)S(1)}, u32[]{:S(2)}, u32[]{:S(2)}) collective-permute-start(bf16[304,256]{1,0:T(8,128)(2,1)S(1)} %get-tuple-element.14), channel_id=1, source_target_pairs={{0,384},{128,0},{256,128},{384,256},{1,385},{129,1},{257,129},{385... | collective-permute-start | bytes 466952 | tf_op jit(solution)/shard_map/ppermute | solution.py:113
  29.8 0.0 collective-permute-done.3.refs_1_
  29.8 1.5 %collective-permute-done.4.refs_2_ = bf16[304,256]{1,0:T(8,128)(2,1)S(1)} collective-permute-done((bf16[304,256]{1,0:T(8,128)(2,1)S(1)}, bf16[304,256]{1,0:T(8,128)(2,1)S(1)}, u32[]{:S(2)}, u32[]{:S(2)}) %collective-permute-start.4) | collective-permute-done | bytes 155680 | tf_op jit(solution)/shard_map/ppermute | solution.py:113
  31.3 2.3 %collective-permute-done.5.refs_3_ = bf16[304,256]{1,0:T(8,128)(2,1)S(1)} collective-permute-done((bf16[304,256]{1,0:T(8,128)(2,1)S(1)}, bf16[304,256]{1,0:T(8,128)(2,1)S(1)}, u32[]{:S(2)}, u32[]{:S(2)}) %collective-permute-start.5) | collective-permute-done | bytes 155680 | tf_op jit(solution)/shard_map/ppermute | solution.py:113
  33.6 1.9 %collective-permute-start.6 = (bf16[4,304,256]{2,1,0:T(8,128)(2,1)S(1)}, bf16[4,304,256]{2,1,0:T(8,128)(2,1)S(1)}, u32[]{:S(2)}, u32[]{:S(2)}) collective-permute-start(bf16[4,304,256]{2,1,0:T(8,128)(2,1)S(1)} %shard_map.57.refs_5_), channel_id=1, source_target_pairs={{0,4},{4,0},{1,5},{5,1},{2,6},{6,2},{3,7},{7,3},{8,12},{12,8},{9,1... | collective-permute-start | bytes 1867784 | tf_op jit(solution)/shard_map/ppermute | solution.py:129
  35.5 0.0 all-to-all-done.refs_0_
  35.5 3.6 %collective-permute-start = (bf16[16,4,2048]{2,1,0:T(4,128)(2,1)S(1)}, bf16[16,4,2048]{2,1,0:T(4,128)(2,1)S(1)}, u32[]{:S(2)}, u32[]{:S(2)}) collective-permute-start(bf16[16,4,2048]{2,1,0:T(4,128)(2,1)S(1)} %all-to-all-done.refs_0_), channel_id=1, source_target_pairs={{0,128},{128,256},{256,384},{384,0},{1,129},{129,257},{257,385},{3... | collective-permute-start | bytes 786440 | tf_op jit(solution)/shard_map/ppermute | solution.py:113
  39.1 4.4 %collective-permute-start.1 = (bf16[16,4,2048]{2,1,0:T(4,128)(2,1)S(1)}, bf16[16,4,2048]{2,1,0:T(4,128)(2,1)S(1)}, u32[]{:S(2)}, u32[]{:S(2)}) collective-permute-start(bf16[16,4,2048]{2,1,0:T(4,128)(2,1)S(1)} %all-to-all-done.refs_0_), channel_id=1, source_target_pairs={{0,256},{128,384},{256,0},{384,128},{1,257},{129,385},{257,1},{385... | collective-permute-start | bytes 786440 | tf_op jit(solution)/shard_map/ppermute | solution.py:113
  43.5 3.3 %collective-permute-start.2 = (bf16[16,4,2048]{2,1,0:T(4,128)(2,1)S(1)}, bf16[16,4,2048]{2,1,0:T(4,128)(2,1)S(1)}, u32[]{:S(2)}, u32[]{:S(2)}) collective-permute-start(bf16[16,4,2048]{2,1,0:T(4,128)(2,1)S(1)} %all-to-all-done.refs_0_), channel_id=1, source_target_pairs={{0,384},{128,0},{256,128},{384,256},{1,385},{129,1},{257,129},{385... | collective-permute-start | bytes 786440 | tf_op jit(solution)/shard_map/ppermute | solution.py:113
  46.8 0.0 copy-start.2
  46.8 0.6 broadcast.6
  47.3 0.1 copy-done.2
  47.4 0.6 reduce.7
  48.1 0.1 reshape.17
  48.2 0.1 convert_reduce_fusion
  48.4 0.1 convert_element_type.7.refs_4_
  48.4 0.0 collective-permute-done.6.refs_6_
  48.5 0.0 collective-permute-done.refs_1_
  48.5 5.4 %collective-permute-done.1.refs_2_ = bf16[16,4,2048]{2,1,0:T(4,128)(2,1)S(1)} collective-permute-done((bf16[16,4,2048]{2,1,0:T(4,128)(2,1)S(1)}, bf16[16,4,2048]{2,1,0:T(4,128)(2,1)S(1)}, u32[]{:S(2)}, u32[]{:S(2)}) %collective-permute-start.1) | collective-permute-done | bytes 262176 | tf_op jit(solution)/shard_map/ppermute | solution.py:113
  53.8 1.7 %collective-permute-done.2.refs_3_ = bf16[16,4,2048]{2,1,0:T(4,128)(2,1)S(1)} collective-permute-done((bf16[16,4,2048]{2,1,0:T(4,128)(2,1)S(1)}, bf16[16,4,2048]{2,1,0:T(4,128)(2,1)S(1)}, u32[]{:S(2)}, u32[]{:S(2)}) %collective-permute-start.2) | collective-permute-done | bytes 262176 | tf_op jit(solution)/shard_map/ppermute | solution.py:113
  55.5 1.4 %shard_map.58 = bf16[16,18,256]{2,1,0:T(8,128)(2,1)S(1)} custom-call(s32[2]{0:T(128)S(1)} %pad_add_fusion.place, bf16[16,4,2048]{2,1,0:T(4,128)(2,1)S(1)} %all-to-all-done.refs_0_, bf16[16,4,2048]{2,1,0:T(4,128)(2,1)S(1)} %collective-permute-done.refs_1_, bf16[16,4,2048]{2,1,0:T(4,128)(2,1)S(1)} %collective-permute-done.1.refs_2_, ...), custom_call_target="tpu_custom_call" | custom-call | tf_op jit(solution)/shard_map/pallas_call | solution.py:133
  56.9 27.9 %all_to_all.10.partials = bf16[16,18,256]{2,1,0:T(8,128)(2,1)S(1)} all-to-all(bf16[16,18,256]{2,1,0:T(8,128)(2,1)S(1)} %shard_map.58), channel_id=1, replica_groups=mesh['x'=4,'z'=16,'core'=2,'y'=4] {'z'}, dimensions={0} | all-to-all | bytes 294912 | tf_op jit(solution)/shard_map/all_to_all | solution.py:137
  84.8 0.7 shard_map.59
  85.5 0.0 copy-start.4
  85.5 1.9 %collective-permute-start.7 = (bf16[9,512]{1,0:T(8,128)(2,1)S(1)}, bf16[9,512]{1,0:T(8,128)(2,1)S(1)}, u32[]{:S(2)}, u32[]{:S(2)}) collective-permute-start(bf16[9,512]{1,0:T(8,128)(2,1)S(1)} %get-tuple-element.16), channel_id=1, source_target_pairs={{0,4},{4,0},{1,5},{5,1},{2,6},{6,2},{3,7},{7,3},{8,12},{12,8},{9,1... | collective-permute-start | bytes 27656 | tf_op jit(solution)/shard_map/ppermute | solution.py:142
  87.4 0.0 copy-done.4
  87.4 0.1 copy.9.abs_
  87.5 1.0 %collective-permute-done.7.got = bf16[9,512]{1,0:T(8,128)(2,1)S(1)} collective-permute-done((bf16[9,512]{1,0:T(8,128)(2,1)S(1)}, bf16[9,512]{1,0:T(8,128)(2,1)S(1)}, u32[]{:S(2)}, u32[]{:S(2)}) %collective-permute-start.7) | collective-permute-done | bytes 9248 | tf_op jit(solution)/shard_map/ppermute | solution.py:142
  88.6 0.7 shard_map.60
  (1 shorter events, 0.0 us)
Async XLA Ops:
  0.0 17.1 %copy-start = (bf16[1152,256]{1,0:T(8,128)(2,1)S(1)}, bf16[1152,256]{1,0:T(8,128)(2,1)}, u32[]{:S(2)}) copy-start(bf16[1152,256]{1,0:T(8,128)(2,1)} %integrals.1) | copy-start | bytes 1769476
  0.0 1.0 %copy-start.1 = (bf16[1,4,32768]{2,1,0:T(4,128)(2,1)S(1)}, bf16[1,4,32768]{2,1,0:T(4,128)(2,1)}, u32[]{:S(2)}) copy-start(bf16[1,4,32768]{2,1,0:T(4,128)(2,1)} %amps.1) | copy-start | bytes 786436
  1.8 33.7 %all-to-all-start = ((bf16[16,4,2048]{2,1,0:T(4,128)(2,1)}), bf16[16,4,2048]{2,1,0:T(4,128)(2,1)S(1)}, u32[]{:S(2)}, u32[]{:S(2)}) async-start(bf16[16,4,2048]{2,1,0:T(4,128)(2,1)} %shard_map.55), calls=%async_computation | async-start | bytes 524288 | tf_op jit(solution)/shard_map/all_to_all | solution.py:125
  17.1 0.7 copy-start.3
  18.4 11.4 %collective-permute-start.3 = (bf16[304,256]{1,0:T(8,128)(2,1)S(1)}, bf16[304,256]{1,0:T(8,128)(2,1)S(1)}, u32[]{:S(2)}, u32[]{:S(2)}) collective-permute-start(bf16[304,256]{1,0:T(8,128)(2,1)S(1)} %get-tuple-element.12), channel_id=1, source_target_pairs={{0,128},{128,256},{256,384},{384,0},{1,129},{129,257},{257,385},{3... | collective-permute-start | bytes 466952 | tf_op jit(solution)/shard_map/ppermute | solution.py:113
  21.8 9.5 %collective-permute-start.4 = (bf16[304,256]{1,0:T(8,128)(2,1)S(1)}, bf16[304,256]{1,0:T(8,128)(2,1)S(1)}, u32[]{:S(2)}, u32[]{:S(2)}) collective-permute-start(bf16[304,256]{1,0:T(8,128)(2,1)S(1)} %get-tuple-element.13), channel_id=1, source_target_pairs={{0,256},{128,384},{256,0},{384,128},{1,257},{129,385},{257,1},{385... | collective-permute-start | bytes 466952 | tf_op jit(solution)/shard_map/ppermute | solution.py:113
  26.4 7.1 %collective-permute-start.5 = (bf16[304,256]{1,0:T(8,128)(2,1)S(1)}, bf16[304,256]{1,0:T(8,128)(2,1)S(1)}, u32[]{:S(2)}, u32[]{:S(2)}) collective-permute-start(bf16[304,256]{1,0:T(8,128)(2,1)S(1)} %get-tuple-element.14), channel_id=1, source_target_pairs={{0,384},{128,0},{256,128},{384,256},{1,385},{129,1},{257,129},{385... | collective-permute-start | bytes 466952 | tf_op jit(solution)/shard_map/ppermute | solution.py:113
  33.6 14.9 %collective-permute-start.6 = (bf16[4,304,256]{2,1,0:T(8,128)(2,1)S(1)}, bf16[4,304,256]{2,1,0:T(8,128)(2,1)S(1)}, u32[]{:S(2)}, u32[]{:S(2)}) collective-permute-start(bf16[4,304,256]{2,1,0:T(8,128)(2,1)S(1)} %shard_map.57.refs_5_), channel_id=1, source_target_pairs={{0,4},{4,0},{1,5},{5,1},{2,6},{6,2},{3,7},{7,3},{8,12},{12,8},{9,1... | collective-permute-start | bytes 1867784 | tf_op jit(solution)/shard_map/ppermute | solution.py:129
  35.5 12.9 %collective-permute-start = (bf16[16,4,2048]{2,1,0:T(4,128)(2,1)S(1)}, bf16[16,4,2048]{2,1,0:T(4,128)(2,1)S(1)}, u32[]{:S(2)}, u32[]{:S(2)}) collective-permute-start(bf16[16,4,2048]{2,1,0:T(4,128)(2,1)S(1)} %all-to-all-done.refs_0_), channel_id=1, source_target_pairs={{0,128},{128,256},{256,384},{384,0},{1,129},{129,257},{257,385},{3... | collective-permute-start | bytes 786440 | tf_op jit(solution)/shard_map/ppermute | solution.py:113
  39.1 14.7 %collective-permute-start.1 = (bf16[16,4,2048]{2,1,0:T(4,128)(2,1)S(1)}, bf16[16,4,2048]{2,1,0:T(4,128)(2,1)S(1)}, u32[]{:S(2)}, u32[]{:S(2)}) collective-permute-start(bf16[16,4,2048]{2,1,0:T(4,128)(2,1)S(1)} %all-to-all-done.refs_0_), channel_id=1, source_target_pairs={{0,256},{128,384},{256,0},{384,128},{1,257},{129,385},{257,1},{385... | collective-permute-start | bytes 786440 | tf_op jit(solution)/shard_map/ppermute | solution.py:113
  43.5 12.0 %collective-permute-start.2 = (bf16[16,4,2048]{2,1,0:T(4,128)(2,1)S(1)}, bf16[16,4,2048]{2,1,0:T(4,128)(2,1)S(1)}, u32[]{:S(2)}, u32[]{:S(2)}) collective-permute-start(bf16[16,4,2048]{2,1,0:T(4,128)(2,1)S(1)} %all-to-all-done.refs_0_), channel_id=1, source_target_pairs={{0,384},{128,0},{256,128},{384,256},{1,385},{129,1},{257,129},{385... | collective-permute-start | bytes 786440 | tf_op jit(solution)/shard_map/ppermute | solution.py:113
  46.8 0.7 copy-start.2
  85.5 1.9 %copy-start.4 = (s32[9]{0:T(128)S(1)}, s32[9]{0:T(128)}, u32[]{:S(2)}) copy-start(s32[9]{0:T(128)} %param.9) | copy-start | bytes 112
  85.5 3.1 %collective-permute-start.7 = (bf16[9,512]{1,0:T(8,128)(2,1)S(1)}, bf16[9,512]{1,0:T(8,128)(2,1)S(1)}, u32[]{:S(2)}, u32[]{:S(2)}) collective-permute-start(bf16[9,512]{1,0:T(8,128)(2,1)S(1)} %get-tuple-element.16), channel_id=1, source_target_pairs={{0,4},{4,0},{1,5},{5,1},{2,6},{6,2},{3,7},{7,3},{8,12},{12,8},{9,1... | collective-permute-start | bytes 27656 | tf_op jit(solution)/shard_map/ppermute | solution.py:142

commit v3 on v0

v3 whole, which is shorter than its diff:
```python
import jax
import jax.numpy as jnp
from jax import lax
from jax.experimental import pallas as pl
from jax.experimental.pallas import tpu as pltpu
from jax.sharding import Mesh, PartitionSpec as P

X, Z, CORES, Y = 4, 16, 2, 4
ROWS = 4
OWN = 9
CDS = 256
AB = X * Z * CORES * OWN
TALL = AB + 16
WIDE = CORES * CDS
LINE = Z * ROWS
HELD = X // 2 * CORES * OWN
BF, F32 = jnp.bfloat16, jnp.float32
HBM = pl.BlockSpec(memory_space=pltpu.HBM)
VMEM = pl.BlockSpec(memory_space=pltpu.VMEM)
SMEM = pl.BlockSpec(memory_space=pltpu.SMEM)


def label_kernel(integrals, labels, labelled):
    labelled[:AB] = integrals[...]
    labelled[AB:] = jnp.broadcast_to(labels[...].astype(F32), (TALL - AB, CDS)).astype(BF)


def regroup_kernel(amps, after, sent):
    for x in range(X):
        for z in range(Z):
            start = (x * Z + z) * WIDE
            sent[z, :, x * WIDE:(x + 1) * WIDE] = amps[0, :, start:start + WIDE]


def multiply_kernel(place, amps, rows, *refs):
    blocks, (out, stacked, acc) = refs[:X * CORES], refs[X * CORES:]
    x, core = place[0], place[1]
    for z in range(Z):
        stacked[z * ROWS:(z + 1) * ROWS, :] = amps[z].astype(F32)
    row_labels = rows[...]
    kept = []
    for c in range(CORES):
        for step in range(X):
            source = lax.rem(x + X - step, X) * CORES + (core if c == 0 else 1 - core)
            values = stacked[:, pl.ds(pl.multiple_of(source * CDS, CDS), CDS)]
            labels = blocks[c * X + step][AB:].astype(F32)[:1]
            kept.append(jnp.where(row_labels == labels, values, jnp.zeros_like(values)).astype(BF))
    tile = 192
    for start in range(0, AB // 2, tile):
        halves = []
        for base in (start, start + AB // 2):
            total = None
            for block, value in zip(blocks, kept):
                term = lax.dot_general(
                    block[base:base + tile], value, (((1,), (1,)), ((), ())), preferred_element_type=F32
                )
                total = term if total is None else total + term
            halves.append(total)
        acc[start:start + tile] = jnp.concatenate(halves, axis=1)
    pairs = CORES * OWN
    for z in range(Z):
        parts = [acc[(k * Z + z) * pairs:(k * Z + z + 1) * pairs, :] for k in range(X // 2)]
        out[z] = jnp.concatenate(parts, axis=0).astype(BF)


def sum_kernel(place, partials, out, total):
    core = place[1]
    value = partials[0].astype(F32)
    for z in range(1, Z):
        value = value + partials[z].astype(F32)
    value = value.astype(BF)
    i = lax.broadcasted_iota(jnp.int32, (2 * LINE, CORES * LINE), 0)
    j = lax.broadcasted_iota(jnp.int32, (2 * LINE, CORES * LINE), 1)
    for half in range(2):
        pair = i - half * LINE
        goal = (pair // ROWS) * (CORES * ROWS) + core * ROWS + lax.rem(i, ROWS)
        spread = jnp.where((j == goal) & (pair >= 0) & (pair < LINE), 1.0, 0.0).astype(BF)
        total[half] = jnp.dot(value, spread, preferred_element_type=F32)
    for k in range(X):
        for c in range(CORES):
            start = (k % 2 * CORES + c) * OWN
            out[k * CORES + c] = total[k // 2, start:start + OWN, :].astype(BF)


def finish_kernel(parts, rows, abs_, out):
    width = CORES * LINE
    for k in range(X):
        lanes = slice(k * width, (k + 1) * width)
        value = parts[k * CORES].astype(F32) + parts[k * CORES + 1].astype(F32)
        keep = rows[:, lanes] == abs_[...]
        out[:, lanes] = jnp.where(keep, value, jnp.zeros_like(value)).astype(BF)


def call(kernel, out_shape, in_specs, scratch=(), cost=None):
    if cost:
        cost = pl.CostEstimate(flops=cost, bytes_accessed=0, transcendentals=0)
    return pl.pallas_call(
        kernel,
        out_shape=out_shape,
        in_specs=in_specs,
        out_specs=jax.tree.map(lambda _: VMEM, out_shape),
        scratch_shapes=list(scratch),
        cost_estimate=cost,
        compiler_params=pltpu.CompilerParams(vmem_limit_bytes=32 * 2**20),
    )


def along_x(value, step):
    return lax.ppermute(value, "x", [(i, (i + step) % X) for i in range(X)])


def body(amplitudes, integrals, pair_irrep, cd_irrep, ab_irrep):
    shape = jax.ShapeDtypeStruct
    core = lax.axis_index("core")
    swap = [(0, 1), (1, 0)]
    place = jnp.stack([lax.axis_index("x"), core]).astype(jnp.int32)
    labelled = call(label_kernel, shape((TALL, CDS), BF), [VMEM, VMEM])(integrals, cd_irrep[None])
    gathered = [labelled] + [along_x(labelled, step) for step in (1, 2, 3)]
    sent = call(
        regroup_kernel, shape((Z, ROWS, X * WIDE), BF), [VMEM, pl.BlockSpec(memory_space=pl.ANY)], cost=None
    )(amplitudes, labelled)
    amps = lax.all_to_all(sent, "z", 0, 0, tiled=True)
    gathered += [lax.ppermute(value, "core", swap) for value in gathered]
    rows = lax.dynamic_slice_in_dim(pair_irrep.reshape(X * Z, CORES, ROWS), lax.axis_index("x") * Z, Z, 0)
    rows = lax.dynamic_slice_in_dim(rows, core, 1, 1)
    rows = rows.reshape(LINE, 1).astype(F32)
    partials = call(
        multiply_kernel, shape((Z, HELD, 2 * LINE), BF), [SMEM] + [VMEM] * (2 + X * CORES),
        [pltpu.VMEM((LINE, X * WIDE), F32), pltpu.VMEM((AB // 2, 2 * LINE), F32)],
    )(place, amps, rows, *gathered)
    partials = lax.all_to_all(partials, "z", 0, 0, tiled=True)
    parts = call(
        sum_kernel, shape((X * CORES, OWN, CORES * LINE), BF), [SMEM, VMEM],
        [pltpu.VMEM((2, HELD, CORES * LINE), F32)],
    )(place, partials)
    parts = lax.all_to_all(parts, ("x", "core"), 0, 0, tiled=True)
    final = shape((OWN, X * CORES * LINE), BF)
    out = call(finish_kernel, final, [VMEM] * 3)(parts, pair_irrep, ab_irrep[:, None])
    return out.T[None]


def solution(mesh):
    split = Mesh(mesh.devices.reshape(X, Z, CORES, Y), ("x", "z", "core", "y"))
    cd = ("x", "z", "core")
    placed = (P("y", cd, None), P(None, cd), P("y", None), P(cd), P(cd))
    return jax.shard_map(body, mesh=split, in_specs=placed, out_specs=P("y", None, cd), check_vma=False)
```

time: 854 us -> 86 us (0.10)
  blocking collectives: 515 us -> 23 us
  other arithmetic: 181 us -> 0.8 us
  local copies, waits for them, and re-layouts: 113 us -> 3.39 us
  starting transfers between devices: 19.8 us -> 39.4 us
  waiting for transfers between devices: 21.8 us -> 12 us
    unnamed x1 -> x0, blocking collectives: 515 us -> none
    unnamed x1, other arithmetic: 179 us -> 0.69 us
    unnamed x14 -> x11, local copies, waits for them, and re-layouts: 82.4 us -> 3.08 us
    all_to_all x2 -> x0, local copies, waits for them, and re-layouts: 30.8 us -> none  [body(): lax.all_to_all(amplitudes, 'cd', split_axis=2, concat_axis=1, tiled=True)[0]]
    all_to_all x0 -> x1, blocking collectives: none -> 23 us  [body(): partials = lax.all_to_all(partials, 'z', 0, 0, tiled=True)]
    ppermute x0 -> x7, starting transfers between devices: none -> 20.2 us  [the longest x3 11.5 us: along_x(): return lax.ppermute(value, 'x', [(i, (i + step) % X) for i in range(X)])]
    all_to_all x1 -> x2, waiting for transfers between devices: 21.8 us -> 11.6 us  [the longest x1 6.88 us: body(): amps = lax.all_to_all(sent, 'z', 0, 0, tiled=True)]
    all_to_all x1 -> x2, starting transfers between devices: 19.8 us -> 19.3 us  [the longest x1 15.2 us: body(): amps = lax.all_to_all(sent, 'z', 0, 0, tiled=True)]
  transfers between devices with their start and end apart: 1 -> 9, of which waited for: 1 -> 3; matrix products, arithmetic and copies ran while one was open for 0% -> 2% of each run, Pallas kernels for 0% -> 1%
where the time goes in v3:
time: 86 us; the launch traced here: 84.7 us
  starting transfers between devices  39.4 us (46%)
  blocking collectives  23 us (27%)
  waiting for transfers between devices  12 us (14%)
  Pallas kernels  5.78 us (7%)
  local copies, waits for them, and re-layouts  3.39 us (4%)
    all_to_all x1, blocking collectives, body(): partials = lax.all_to_all(partials, 'z', 0, 0, tiled=True)  23 us
    all_to_all x1, starting transfers between devices, body(): amps = lax.all_to_all(sent, 'z', 0, 0, tiled=True)  15.2 us
    ppermute x3, starting transfers between devices, along_x(): return lax.ppermute(value, 'x', [(i, (i + step) % X) for i in range(X)])  11.5 us
    ppermute x4, starting transfers between devices, body(): gathered += [lax.ppermute(value, 'core', swap) for value in gathered]  8.65 us
    all_to_all x1, waiting for transfers between devices, body(): amps = lax.all_to_all(sent, 'z', 0, 0, tiled=True)  6.88 us
    all_to_all x1, waiting for transfers between devices, body(): parts = lax.all_to_all(parts, ('x', 'core'), 0, 0, tiled=True)  4.7 us
    all_to_all x1, starting transfers between devices, body(): parts = lax.all_to_all(parts, ('x', 'core'), 0, 0, tiled=True)  4.09 us
    unnamed x11, local copies, waits for them, and re-layouts  3.08 us
  transfers between devices with their start and end apart: 9, of which 3 were waited for; matrix products, arithmetic and copies ran while one was open for 2% of the time, Pallas kernels for 1%

profile of v3, /device:TPU:24, one launch (start us, length us, event | category | flops | bytes accessed | tf_op | source)
XLA Modules:
  0.0 84.7 jit_solution(16972258438863473955)
XLA Ops:
  0.0 0.0 copy-start.3
  0.0 0.7 copy-done.3
  0.7 0.0 copy-start
  0.7 1.1 %copy-done = bf16[1152,256]{1,0:T(8,128)(2,1)S(1)} copy-done((bf16[1152,256]{1,0:T(8,128)(2,1)S(1)}, bf16[1152,256]{1,0:T(8,128)(2,1)}, u32[]{:S(2)}) %copy-start) | copy-done | bytes 589848
  1.7 0.0 copy-start.1
  1.8 3.5 %collective-permute-start = (bf16[1168,256]{1,0:T(8,128)(2,1)S(1)}, bf16[1168,256]{1,0:T(8,128)(2,1)S(1)}, u32[]{:S(2)}, u32[]{:S(2)}) collective-permute-start(bf16[1168,256]{1,0:T(8,128)(2,1)S(1)} %shard_map.55.after.refs_0_), channel_id=1, source_target_pairs={{0,128},{128,256},{256,384},{384,0},{1,129},{129,257},{257,385},{3... | collective-permute-start | bytes 1794056 | tf_op jit(solution)/shard_map/ppermute | solution.py:109
  5.3 4.6 %collective-permute-start.1 = (bf16[1168,256]{1,0:T(8,128)(2,1)S(1)}, bf16[1168,256]{1,0:T(8,128)(2,1)S(1)}, u32[]{:S(2)}, u32[]{:S(2)}) collective-permute-start(bf16[1168,256]{1,0:T(8,128)(2,1)S(1)} %shard_map.55.after.refs_0_), channel_id=1, source_target_pairs={{0,256},{128,384},{256,0},{384,128},{1,257},{129,385},{257,1},{385... | collective-permute-start | bytes 1794056 | tf_op jit(solution)/shard_map/ppermute | solution.py:109
  10.0 3.3 %collective-permute-start.2 = (bf16[1168,256]{1,0:T(8,128)(2,1)S(1)}, bf16[1168,256]{1,0:T(8,128)(2,1)S(1)}, u32[]{:S(2)}, u32[]{:S(2)}) collective-permute-start(bf16[1168,256]{1,0:T(8,128)(2,1)S(1)} %shard_map.55.after.refs_0_), channel_id=1, source_target_pairs={{0,384},{128,0},{256,128},{384,256},{1,385},{129,1},{257,129},{385... | collective-permute-start | bytes 1794056 | tf_op jit(solution)/shard_map/ppermute | solution.py:109
  13.3 0.0 copy-done.1
  13.3 0.7 shard_map.56
  14.1 15.2 %all-to-all-start = ((bf16[16,4,2048]{2,1,0:T(4,128)(2,1)}), bf16[16,4,2048]{2,1,0:T(4,128)(2,1)S(1)}, u32[]{:S(2)}, u32[]{:S(2)}) async-start(bf16[16,4,2048]{2,1,0:T(4,128)(2,1)} %shard_map.56), calls=%async_computation | async-start | bytes 524288 | tf_op jit(solution)/shard_map/all_to_all | solution.py:122
  29.3 1.9 %collective-permute-start.3 = (bf16[1168,256]{1,0:T(8,128)(2,1)S(1)}, bf16[1168,256]{1,0:T(8,128)(2,1)S(1)}, u32[]{:S(2)}, u32[]{:S(2)}) collective-permute-start(bf16[1168,256]{1,0:T(8,128)(2,1)S(1)} %shard_map.55.after.refs_0_), channel_id=1, source_target_pairs={{0,4},{4,0},{1,5},{5,1},{2,6},{6,2},{3,7},{7,3},{8,12},{12,8},{9,1... | collective-permute-start | bytes 1794056 | tf_op jit(solution)/shard_map/ppermute | solution.py:123
  31.2 0.0 collective-permute-done.refs_1_
  31.2 2.4 %collective-permute-start.4 = (bf16[1168,256]{1,0:T(8,128)(2,1)S(1)}, bf16[1168,256]{1,0:T(8,128)(2,1)}, u32[]{:S(2)}, u32[]{:S(2)}) collective-permute-start(bf16[1168,256]{1,0:T(8,128)(2,1)S(1)} %collective-permute-done.refs_1_), channel_id=1, source_target_pairs={{0,4},{4,0},{1,5},{5,1},{2,6},{6,2},{3,7},{7,3},{8,12},{12,8},{9,1... | collective-permute-start | bytes 1794056 | tf_op jit(solution)/shard_map/ppermute | solution.py:123
  33.6 0.4 collective-permute-done.1.refs_2_
  34.1 1.9 %collective-permute-start.5 = (bf16[1168,256]{1,0:T(8,128)(2,1)S(1)}, bf16[1168,256]{1,0:T(8,128)(2,1)}, u32[]{:S(2)}, u32[]{:S(2)}) collective-permute-start(bf16[1168,256]{1,0:T(8,128)(2,1)S(1)} %collective-permute-done.1.refs_2_), channel_id=1, source_target_pairs={{0,4},{4,0},{1,5},{5,1},{2,6},{6,2},{3,7},{7,3},{8,12},{12,8},{9,1... | collective-permute-start | bytes 1794056 | tf_op jit(solution)/shard_map/ppermute | solution.py:123
  36.0 0.0 collective-permute-done.2.refs_3_
  36.0 2.4 %collective-permute-start.6 = (bf16[1168,256]{1,0:T(8,128)(2,1)S(1)}, bf16[1168,256]{1,0:T(8,128)(2,1)}, u32[]{:S(2)}, u32[]{:S(2)}) collective-permute-start(bf16[1168,256]{1,0:T(8,128)(2,1)S(1)} %collective-permute-done.2.refs_3_), channel_id=1, source_target_pairs={{0,4},{4,0},{1,5},{5,1},{2,6},{6,2},{3,7},{7,3},{8,12},{12,8},{9,1... | collective-permute-start | bytes 1794056 | tf_op jit(solution)/shard_map/ppermute | solution.py:123
  38.4 0.0 copy-start.2
  38.4 0.6 broadcast.6
  39.0 0.1 copy-done.2
  39.1 0.7 reduce.7
  39.8 0.1 reshape.17
  40.0 0.1 convert_element_type.7.rows
  40.1 0.1 pad_add_fusion.place
  40.2 0.0 collective-permute-done.3.refs_4_
  40.2 6.9 %all-to-all-done.amps = bf16[16,4,2048]{2,1,0:T(4,128)(2,1)S(1)} async-done(((bf16[16,4,2048]{2,1,0:T(4,128)(2,1)}), bf16[16,4,2048]{2,1,0:T(4,128)(2,1)S(1)}, u32[]{:S(2)}, u32[]{:S(2)}) %all-to-all-start) | async-done | bytes 262176 | tf_op jit(solution)/shard_map/all_to_all | solution.py:122
  47.0 0.0 collective-permute-done.4.refs_5_
  47.0 0.0 collective-permute-done.5.refs_6_
  47.0 0.0 collective-permute-done.6.refs_7_
  47.1 3.0 %shard_map.57 = bf16[16,36,128]{2,1,0:T(8,128)(2,1)S(1)} custom-call(s32[2]{0:T(128)S(1)} %pad_add_fusion.place, bf16[16,4,2048]{2,1,0:T(4,128)(2,1)S(1)} %all-to-all-done.amps, f32[64,1]{1,0:T(8,128)S(1)} %convert_element_type.7.rows, bf16[1168,256]{1,0:T(8,128)(2,1)S(1)} %shard_map.55.after.refs_0_, bf16[1168,256]{1,0:T(8,128)(2,1)S(1)} %collective-permute-done.refs_1_, ...), custom_call_target="tpu_custom_call" | custom-call | tf_op jit(solution)/shard_map/pallas_call | solution.py:127
  50.1 23.0 %all_to_all.15.partials = bf16[16,36,128]{2,1,0:T(8,128)(2,1)S(1)} all-to-all(bf16[16,36,128]{2,1,0:T(8,128)(2,1)S(1)} %shard_map.57), channel_id=1, replica_groups=mesh['x'=4,'z'=16,'core'=2,'y'=4] {'z'}, dimensions={0} | all-to-all | bytes 294912 | tf_op jit(solution)/shard_map/all_to_all | solution.py:131
  73.1 1.3 %shard_map.58 = bf16[8,9,128]{2,1,0:T(8,128)(2,1)} custom-call(s32[2]{0:T(128)S(1)} %pad_add_fusion.place, bf16[16,36,128]{2,1,0:T(8,128)(2,1)S(1)} %all_to_all.15.partials), custom_call_target="tpu_custom_call" | custom-call | tf_op jit(solution)/shard_map/pallas_call | solution.py:132
  74.4 4.1 %all-to-all-start.2 = ((bf16[8,9,128]{2,1,0:T(8,128)(2,1)}), bf16[8,9,128]{2,1,0:T(8,128)(2,1)S(1)}, u32[]{:S(2)}, u32[]{:S(2)}) async-start(bf16[8,9,128]{2,1,0:T(8,128)(2,1)} %shard_map.58), calls=%async_computation.2 | async-start | bytes 65536 | tf_op jit(solution)/shard_map/all_to_all | solution.py:136
  78.5 0.0 copy-start.4
  78.5 0.7 copy-done.4
  79.2 0.1 copy.10.abs_
  79.3 4.7 %all-to-all-done.2.parts = bf16[8,9,128]{2,1,0:T(8,128)(2,1)S(1)} async-done(((bf16[8,9,128]{2,1,0:T(8,128)(2,1)}), bf16[8,9,128]{2,1,0:T(8,128)(2,1)S(1)}, u32[]{:S(2)}, u32[]{:S(2)}) %all-to-all-start.2) | async-done | bytes 18464 | tf_op jit(solution)/shard_map/all_to_all | solution.py:136
  84.0 0.7 shard_map.59
  (2 shorter events, 0.1 us)
Async XLA Ops:
  0.0 0.7 copy-start.3
  0.7 1.1 %copy-start = (bf16[1152,256]{1,0:T(8,128)(2,1)S(1)}, bf16[1152,256]{1,0:T(8,128)(2,1)}, u32[]{:S(2)}) copy-start(bf16[1152,256]{1,0:T(8,128)(2,1)} %integrals.1) | copy-start | bytes 1769476
  1.7 11.6 %copy-start.1 = (bf16[1,4,32768]{2,1,0:T(4,128)(2,1)S(1)}, bf16[1,4,32768]{2,1,0:T(4,128)(2,1)}, u32[]{:S(2)}) copy-start(bf16[1,4,32768]{2,1,0:T(4,128)(2,1)} %amps.1) | copy-start | bytes 786436
  1.8 29.4 %collective-permute-start = (bf16[1168,256]{1,0:T(8,128)(2,1)S(1)}, bf16[1168,256]{1,0:T(8,128)(2,1)S(1)}, u32[]{:S(2)}, u32[]{:S(2)}) collective-permute-start(bf16[1168,256]{1,0:T(8,128)(2,1)S(1)} %shard_map.55.after.refs_0_), channel_id=1, source_target_pairs={{0,128},{128,256},{256,384},{384,0},{1,129},{129,257},{257,385},{3... | collective-permute-start | bytes 1794056 | tf_op jit(solution)/shard_map/ppermute | solution.py:109
  5.3 28.7 %collective-permute-start.1 = (bf16[1168,256]{1,0:T(8,128)(2,1)S(1)}, bf16[1168,256]{1,0:T(8,128)(2,1)S(1)}, u32[]{:S(2)}, u32[]{:S(2)}) collective-permute-start(bf16[1168,256]{1,0:T(8,128)(2,1)S(1)} %shard_map.55.after.refs_0_), channel_id=1, source_target_pairs={{0,256},{128,384},{256,0},{384,128},{1,257},{129,385},{257,1},{385... | collective-permute-start | bytes 1794056 | tf_op jit(solution)/shard_map/ppermute | solution.py:109
  10.0 26.0 %collective-permute-start.2 = (bf16[1168,256]{1,0:T(8,128)(2,1)S(1)}, bf16[1168,256]{1,0:T(8,128)(2,1)S(1)}, u32[]{:S(2)}, u32[]{:S(2)}) collective-permute-start(bf16[1168,256]{1,0:T(8,128)(2,1)S(1)} %shard_map.55.after.refs_0_), channel_id=1, source_target_pairs={{0,384},{128,0},{256,128},{384,256},{1,385},{129,1},{257,129},{385... | collective-permute-start | bytes 1794056 | tf_op jit(solution)/shard_map/ppermute | solution.py:109
  14.1 33.0 %all-to-all-start = ((bf16[16,4,2048]{2,1,0:T(4,128)(2,1)}), bf16[16,4,2048]{2,1,0:T(4,128)(2,1)S(1)}, u32[]{:S(2)}, u32[]{:S(2)}) async-start(bf16[16,4,2048]{2,1,0:T(4,128)(2,1)} %shard_map.56), calls=%async_computation | async-start | bytes 524288 | tf_op jit(solution)/shard_map/all_to_all | solution.py:122
  29.3 10.9 %collective-permute-start.3 = (bf16[1168,256]{1,0:T(8,128)(2,1)S(1)}, bf16[1168,256]{1,0:T(8,128)(2,1)S(1)}, u32[]{:S(2)}, u32[]{:S(2)}) collective-permute-start(bf16[1168,256]{1,0:T(8,128)(2,1)S(1)} %shard_map.55.after.refs_0_), channel_id=1, source_target_pairs={{0,4},{4,0},{1,5},{5,1},{2,6},{6,2},{3,7},{7,3},{8,12},{12,8},{9,1... | collective-permute-start | bytes 1794056 | tf_op jit(solution)/shard_map/ppermute | solution.py:123
  31.2 15.8 %collective-permute-start.4 = (bf16[1168,256]{1,0:T(8,128)(2,1)S(1)}, bf16[1168,256]{1,0:T(8,128)(2,1)}, u32[]{:S(2)}, u32[]{:S(2)}) collective-permute-start(bf16[1168,256]{1,0:T(8,128)(2,1)S(1)} %collective-permute-done.refs_1_), channel_id=1, source_target_pairs={{0,4},{4,0},{1,5},{5,1},{2,6},{6,2},{3,7},{7,3},{8,12},{12,8},{9,1... | collective-permute-start | bytes 1794056 | tf_op jit(solution)/shard_map/ppermute | solution.py:123
  34.1 13.0 %collective-permute-start.5 = (bf16[1168,256]{1,0:T(8,128)(2,1)S(1)}, bf16[1168,256]{1,0:T(8,128)(2,1)}, u32[]{:S(2)}, u32[]{:S(2)}) collective-permute-start(bf16[1168,256]{1,0:T(8,128)(2,1)S(1)} %collective-permute-done.1.refs_2_), channel_id=1, source_target_pairs={{0,4},{4,0},{1,5},{5,1},{2,6},{6,2},{3,7},{7,3},{8,12},{12,8},{9,1... | collective-permute-start | bytes 1794056 | tf_op jit(solution)/shard_map/ppermute | solution.py:123
  36.0 11.1 %collective-permute-start.6 = (bf16[1168,256]{1,0:T(8,128)(2,1)S(1)}, bf16[1168,256]{1,0:T(8,128)(2,1)}, u32[]{:S(2)}, u32[]{:S(2)}) collective-permute-start(bf16[1168,256]{1,0:T(8,128)(2,1)S(1)} %collective-permute-done.2.refs_3_), channel_id=1, source_target_pairs={{0,4},{4,0},{1,5},{5,1},{2,6},{6,2},{3,7},{7,3},{8,12},{12,8},{9,1... | collective-permute-start | bytes 1794056 | tf_op jit(solution)/shard_map/ppermute | solution.py:123
  38.4 0.7 copy-start.2
  74.4 9.5 %all-to-all-start.2 = ((bf16[8,9,128]{2,1,0:T(8,128)(2,1)}), bf16[8,9,128]{2,1,0:T(8,128)(2,1)S(1)}, u32[]{:S(2)}, u32[]{:S(2)}) async-start(bf16[8,9,128]{2,1,0:T(8,128)(2,1)} %shard_map.58), calls=%async_computation.2 | async-start | bytes 65536 | tf_op jit(solution)/shard_map/all_to_all | solution.py:136
  78.5 0.7 copy-start.4

commit v4 on v3

--- a/solution.py
+++ b/solution.py
@@ -20,11 +20,6 @@
 SMEM = pl.BlockSpec(memory_space=pltpu.SMEM)
 
 
-def label_kernel(integrals, labels, labelled):
-    labelled[:AB] = integrals[...]
-    labelled[AB:] = jnp.broadcast_to(labels[...].astype(F32), (TALL - AB, CDS)).astype(BF)
-
-
 def regroup_kernel(amps, after, sent):
     for x in range(X):
         for z in range(Z):
@@ -41,7 +36,7 @@
     kept = []
     for c in range(CORES):
         for step in range(X):
-            source = lax.rem(x + X - step, X) * CORES + (core if c == 0 else 1 - core)
+            source = lax.rem(x + X - (0, 2, 1, 3)[step], X) * CORES + (core if c == 0 else 1 - core)
             values = stacked[:, pl.ds(pl.multiple_of(source * CDS, CDS), CDS)]
             labels = blocks[c * X + step][AB:].astype(F32)[:1]
             kept.append(jnp.where(row_labels == labels, values, jnp.zeros_like(values)).astype(BF))
@@ -114,8 +109,9 @@
     core = lax.axis_index("core")
     swap = [(0, 1), (1, 0)]
     place = jnp.stack([lax.axis_index("x"), core]).astype(jnp.int32)
-    labelled = call(label_kernel, shape((TALL, CDS), BF), [VMEM, VMEM])(integrals, cd_irrep[None])
-    gathered = [labelled] + [along_x(labelled, step) for step in (1, 2, 3)]
+    irreps = jnp.broadcast_to(cd_irrep[None].astype(BF), (TALL - AB, CDS))
+    labelled = jnp.concatenate([integrals, irreps], axis=0)
+    gathered = [labelled] + [along_x(labelled, step) for step in (2, 1, 3)]
     sent = call(
         regroup_kernel, shape((Z, ROWS, X * WIDE), BF), [VMEM, pl.BlockSpec(memory_space=pl.ANY)], cost=None
     )(amplitudes, labelled)

time: 86 us -> 85.4 us (level)
  local copies, waits for them, and re-layouts: 3.39 us -> 0.91 us
  other arithmetic: 0.8 us -> 2.59 us
  blocking collectives: 23 us -> 21.7 us
    unnamed x11 -> x7, local copies, waits for them, and re-layouts: 3.08 us -> 0.59 us
    all_to_all x1, blocking collectives: 23 us -> 21.7 us  [body(): partials = lax.all_to_all(partials, 'z', 0, 0, tiled=True)]
    concatenate x0 -> x1, other arithmetic: none -> 1.15 us  [body(): labelled = jnp.concatenate([integrals, irreps], axis=0)]
  transfers between devices with their start and end apart: 9 -> 9, of which waited for: 3 -> 2; matrix products, arithmetic and copies ran while one was open for 2% -> 2% of each run, Pallas kernels for 1% -> 1%
where the time goes in v4:
time: 85.4 us; the launch traced here: 84.1 us
  starting transfers between devices  40.1 us (47%)
  blocking collectives  21.7 us (25%)
  waiting for transfers between devices  12.8 us (15%)
  Pallas kernels  5.72 us (7%)
  other arithmetic  2.59 us (3%)
  local copies, waits for them, and re-layouts  0.91 us (1%)
    all_to_all x1, blocking collectives, body(): partials = lax.all_to_all(partials, 'z', 0, 0, tiled=True)  21.7 us
    all_to_all x1, starting transfers between devices, body(): amps = lax.all_to_all(sent, 'z', 0, 0, tiled=True)  15.2 us
    ppermute x3, starting transfers between devices, along_x(): return lax.ppermute(value, 'x', [(i, (i + step) % X) for i in range(X)])  12 us
    ppermute x4, starting transfers between devices, body(): gathered += [lax.ppermute(value, 'core', swap) for value in gathered]  8.66 us
    all_to_all x1, waiting for transfers between devices, body(): amps = lax.all_to_all(sent, 'z', 0, 0, tiled=True)  7.44 us
    all_to_all x1, waiting for transfers between devices, body(): parts = lax.all_to_all(parts, ('x', 'core'), 0, 0, tiled=True)  5.35 us
    all_to_all x1, starting transfers between devices, body(): parts = lax.all_to_all(parts, ('x', 'core'), 0, 0, tiled=True)  4.3 us
    pallas_call x1, Pallas kernels, body(): call(multiply_kernel, shape((Z, HELD, 2 * LINE), BF), [SMEM] + [VMEM] * (...  2.99 us
  transfers between devices with their start and end apart: 9, of which 2 were waited for; matrix products, arithmetic and copies ran while one was open for 2% of the time, Pallas kernels for 1%

profile of v4, /device:TPU:24, one launch (start us, length us, event | category | flops | bytes accessed | tf_op | source)
XLA Modules:
  0.0 84.1 jit_solution(8812186069852004480)
XLA Ops:
  0.0 0.7 convert_element_type.9
  0.7 0.0 copy-start
  0.7 1.1 %pad_maximum_fusion.after.refs_0_ = bf16[1168,256]{1,0:T(8,128)(2,1)S(1)} fusion(bf16[16,256]{1,0:T(8,128)(2,1)S(1)} %broadcast_in_dim.12, bf16[1152,256]{1,0:T(8,128)(2,1)} %param.6), kind=kLoop, calls=%fused_computation | loop fusion | flops 1196032 | bytes 1196032 | tf_op jit(solution)/shard_map/concatenate | solution.py:113
  1.8 0.0 copy-start.1
  1.9 4.9 %collective-permute-start = (bf16[1168,256]{1,0:T(8,128)(2,1)S(1)}, bf16[1168,256]{1,0:T(8,128)(2,1)S(1)}, u32[]{:S(2)}, u32[]{:S(2)}) collective-permute-start(bf16[1168,256]{1,0:T(8,128)(2,1)S(1)} %pad_maximum_fusion.after.refs_0_), channel_id=1, source_target_pairs={{0,256},{128,384},{256,0},{384,128},{1,257},{129,385},{257,1},{385... | collective-permute-start | bytes 1794056 | tf_op jit(solution)/shard_map/ppermute | solution.py:104
  6.8 2.5 %collective-permute-start.1 = (bf16[1168,256]{1,0:T(8,128)(2,1)S(1)}, bf16[1168,256]{1,0:T(8,128)(2,1)S(1)}, u32[]{:S(2)}, u32[]{:S(2)}) collective-permute-start(bf16[1168,256]{1,0:T(8,128)(2,1)S(1)} %pad_maximum_fusion.after.refs_0_), channel_id=1, source_target_pairs={{0,128},{128,256},{256,384},{384,0},{1,129},{129,257},{257,385},{3... | collective-permute-start | bytes 1794056 | tf_op jit(solution)/shard_map/ppermute | solution.py:104
  9.3 4.6 %collective-permute-start.2 = (bf16[1168,256]{1,0:T(8,128)(2,1)S(1)}, bf16[1168,256]{1,0:T(8,128)(2,1)S(1)}, u32[]{:S(2)}, u32[]{:S(2)}) collective-permute-start(bf16[1168,256]{1,0:T(8,128)(2,1)S(1)} %pad_maximum_fusion.after.refs_0_), channel_id=1, source_target_pairs={{0,384},{128,0},{256,128},{384,256},{1,385},{129,1},{257,129},{385... | collective-permute-start | bytes 1794056 | tf_op jit(solution)/shard_map/ppermute | solution.py:104
  13.9 0.0 copy-done
  13.9 0.7 shard_map.55
  14.6 15.2 %all-to-all-start = ((bf16[16,4,2048]{2,1,0:T(4,128)(2,1)}), bf16[16,4,2048]{2,1,0:T(4,128)(2,1)S(1)}, u32[]{:S(2)}, u32[]{:S(2)}) async-start(bf16[16,4,2048]{2,1,0:T(4,128)(2,1)} %shard_map.55), calls=%async_computation | async-start | bytes 524288 | tf_op jit(solution)/shard_map/all_to_all | solution.py:118
  29.8 1.9 %collective-permute-start.3 = (bf16[1168,256]{1,0:T(8,128)(2,1)S(1)}, bf16[1168,256]{1,0:T(8,128)(2,1)S(1)}, u32[]{:S(2)}, u32[]{:S(2)}) collective-permute-start(bf16[1168,256]{1,0:T(8,128)(2,1)S(1)} %pad_maximum_fusion.after.refs_0_), channel_id=1, source_target_pairs={{0,4},{4,0},{1,5},{5,1},{2,6},{6,2},{3,7},{7,3},{8,12},{12,8},{9,1... | collective-permute-start | bytes 1794056 | tf_op jit(solution)/shard_map/ppermute | solution.py:119
  31.7 0.0 collective-permute-done.refs_1_
  31.7 2.4 %collective-permute-start.4 = (bf16[1168,256]{1,0:T(8,128)(2,1)S(1)}, bf16[1168,256]{1,0:T(8,128)(2,1)}, u32[]{:S(2)}, u32[]{:S(2)}) collective-permute-start(bf16[1168,256]{1,0:T(8,128)(2,1)S(1)} %collective-permute-done.refs_1_), channel_id=1, source_target_pairs={{0,4},{4,0},{1,5},{5,1},{2,6},{6,2},{3,7},{7,3},{8,12},{12,8},{9,1... | collective-permute-start | bytes 1794056 | tf_op jit(solution)/shard_map/ppermute | solution.py:119
  34.2 0.0 collective-permute-done.1.refs_2_
  34.2 1.9 %collective-permute-start.5 = (bf16[1168,256]{1,0:T(8,128)(2,1)S(1)}, bf16[1168,256]{1,0:T(8,128)(2,1)}, u32[]{:S(2)}, u32[]{:S(2)}) collective-permute-start(bf16[1168,256]{1,0:T(8,128)(2,1)S(1)} %collective-permute-done.1.refs_2_), channel_id=1, source_target_pairs={{0,4},{4,0},{1,5},{5,1},{2,6},{6,2},{3,7},{7,3},{8,12},{12,8},{9,1... | collective-permute-start | bytes 1794056 | tf_op jit(solution)/shard_map/ppermute | solution.py:119
  36.1 0.0 collective-permute-done.2.refs_3_
  36.1 2.4 %collective-permute-start.6 = (bf16[1168,256]{1,0:T(8,128)(2,1)S(1)}, bf16[1168,256]{1,0:T(8,128)(2,1)}, u32[]{:S(2)}, u32[]{:S(2)}) collective-permute-start(bf16[1168,256]{1,0:T(8,128)(2,1)S(1)} %collective-permute-done.2.refs_3_), channel_id=1, source_target_pairs={{0,4},{4,0},{1,5},{5,1},{2,6},{6,2},{3,7},{7,3},{8,12},{12,8},{9,1... | collective-permute-start | bytes 1794056 | tf_op jit(solution)/shard_map/ppermute | solution.py:119
  38.5 0.6 broadcast.7
  39.1 0.0 copy-done.1
  39.1 0.7 reduce.7
  39.8 0.1 reshape.19
  40.0 0.1 convert_element_type.12.rows
  40.0 0.1 pad_add_fusion.place
  40.1 0.0 copy-start.2
  40.1 0.0 collective-permute-done.3.refs_4_
  40.1 7.4 %all-to-all-done.amps = bf16[16,4,2048]{2,1,0:T(4,128)(2,1)S(1)} async-done(((bf16[16,4,2048]{2,1,0:T(4,128)(2,1)}), bf16[16,4,2048]{2,1,0:T(4,128)(2,1)S(1)}, u32[]{:S(2)}, u32[]{:S(2)}) %all-to-all-start) | async-done | bytes 262176 | tf_op jit(solution)/shard_map/all_to_all | solution.py:118
  47.6 0.0 collective-permute-done.4.refs_5_
  47.6 0.0 collective-permute-done.5.refs_6_
  47.6 0.0 collective-permute-done.6.refs_7_
  47.6 3.0 %shard_map.56 = bf16[16,36,128]{2,1,0:T(8,128)(2,1)S(1)} custom-call(s32[2]{0:T(128)S(1)} %pad_add_fusion.place, bf16[16,4,2048]{2,1,0:T(4,128)(2,1)S(1)} %all-to-all-done.amps, f32[64,1]{1,0:T(8,128)S(1)} %convert_element_type.12.rows, bf16[1168,256]{1,0:T(8,128)(2,1)S(1)} %pad_maximum_fusion.after.refs_0_, ...), custom_call_target="tpu_custom_call" | custom-call | tf_op jit(solution)/shard_map/pallas_call | solution.py:123
  50.6 21.7 %all_to_all.15.partials = bf16[16,36,128]{2,1,0:T(8,128)(2,1)S(1)} all-to-all(bf16[16,36,128]{2,1,0:T(8,128)(2,1)S(1)} %shard_map.56), channel_id=1, replica_groups=mesh['x'=4,'z'=16,'core'=2,'y'=4] {'z'}, dimensions={0} | all-to-all | bytes 294912 | tf_op jit(solution)/shard_map/all_to_all | solution.py:127
  72.3 1.3 %shard_map.57 = bf16[8,9,128]{2,1,0:T(8,128)(2,1)} custom-call(s32[2]{0:T(128)S(1)} %pad_add_fusion.place, bf16[16,36,128]{2,1,0:T(8,128)(2,1)S(1)} %all_to_all.15.partials), custom_call_target="tpu_custom_call" | custom-call | tf_op jit(solution)/shard_map/pallas_call | solution.py:128
  73.6 4.3 %all-to-all-start.2 = ((bf16[8,9,128]{2,1,0:T(8,128)(2,1)}), bf16[8,9,128]{2,1,0:T(8,128)(2,1)S(1)}, u32[]{:S(2)}, u32[]{:S(2)}) async-start(bf16[8,9,128]{2,1,0:T(8,128)(2,1)} %shard_map.57), calls=%async_computation.2 | async-start | bytes 65536 | tf_op jit(solution)/shard_map/all_to_all | solution.py:132
  77.9 0.0 copy-done.2
  77.9 0.1 copy.10.abs_
  78.0 5.3 %all-to-all-done.2.parts = bf16[8,9,128]{2,1,0:T(8,128)(2,1)S(1)} async-done(((bf16[8,9,128]{2,1,0:T(8,128)(2,1)}), bf16[8,9,128]{2,1,0:T(8,128)(2,1)S(1)}, u32[]{:S(2)}, u32[]{:S(2)}) %all-to-all-start.2) | async-done | bytes 18464 | tf_op jit(solution)/shard_map/all_to_all | solution.py:132
  83.4 0.7 shard_map.58
  (2 shorter events, 0.0 us)
Async XLA Ops:
  0.7 13.2 %copy-start = (bf16[1,4,32768]{2,1,0:T(4,128)(2,1)S(1)}, bf16[1,4,32768]{2,1,0:T(4,128)(2,1)}, u32[]{:S(2)}) copy-start(bf16[1,4,32768]{2,1,0:T(4,128)(2,1)} %amps.1) | copy-start | bytes 786436
  1.8 37.3 %copy-start.1 = (s32[1,512]{1,0:T(1,128)S(1)}, s32[1,512]{1,0:T(1,128)}, u32[]{:S(2)}) copy-start(s32[1,512]{1,0:T(1,128)} %rows.1) | copy-start | bytes 6148
  1.9 29.9 %collective-permute-start = (bf16[1168,256]{1,0:T(8,128)(2,1)S(1)}, bf16[1168,256]{1,0:T(8,128)(2,1)S(1)}, u32[]{:S(2)}, u32[]{:S(2)}) collective-permute-start(bf16[1168,256]{1,0:T(8,128)(2,1)S(1)} %pad_maximum_fusion.after.refs_0_), channel_id=1, source_target_pairs={{0,256},{128,384},{256,0},{384,128},{1,257},{129,385},{257,1},{385... | collective-permute-start | bytes 1794056 | tf_op jit(solution)/shard_map/ppermute | solution.py:104
  6.8 27.4 %collective-permute-start.1 = (bf16[1168,256]{1,0:T(8,128)(2,1)S(1)}, bf16[1168,256]{1,0:T(8,128)(2,1)S(1)}, u32[]{:S(2)}, u32[]{:S(2)}) collective-permute-start(bf16[1168,256]{1,0:T(8,128)(2,1)S(1)} %pad_maximum_fusion.after.refs_0_), channel_id=1, source_target_pairs={{0,128},{128,256},{256,384},{384,0},{1,129},{129,257},{257,385},{3... | collective-permute-start | bytes 1794056 | tf_op jit(solution)/shard_map/ppermute | solution.py:104
  9.3 26.8 %collective-permute-start.2 = (bf16[1168,256]{1,0:T(8,128)(2,1)S(1)}, bf16[1168,256]{1,0:T(8,128)(2,1)S(1)}, u32[]{:S(2)}, u32[]{:S(2)}) collective-permute-start(bf16[1168,256]{1,0:T(8,128)(2,1)S(1)} %pad_maximum_fusion.after.refs_0_), channel_id=1, source_target_pairs={{0,384},{128,0},{256,128},{384,256},{1,385},{129,1},{257,129},{385... | collective-permute-start | bytes 1794056 | tf_op jit(solution)/shard_map/ppermute | solution.py:104
  14.6 33.0 %all-to-all-start = ((bf16[16,4,2048]{2,1,0:T(4,128)(2,1)}), bf16[16,4,2048]{2,1,0:T(4,128)(2,1)S(1)}, u32[]{:S(2)}, u32[]{:S(2)}) async-start(bf16[16,4,2048]{2,1,0:T(4,128)(2,1)} %shard_map.55), calls=%async_computation | async-start | bytes 524288 | tf_op jit(solution)/shard_map/all_to_all | solution.py:118
  29.8 10.3 %collective-permute-start.3 = (bf16[1168,256]{1,0:T(8,128)(2,1)S(1)}, bf16[1168,256]{1,0:T(8,128)(2,1)S(1)}, u32[]{:S(2)}, u32[]{:S(2)}) collective-permute-start(bf16[1168,256]{1,0:T(8,128)(2,1)S(1)} %pad_maximum_fusion.after.refs_0_), channel_id=1, source_target_pairs={{0,4},{4,0},{1,5},{5,1},{2,6},{6,2},{3,7},{7,3},{8,12},{12,8},{9,1... | collective-permute-start | bytes 1794056 | tf_op jit(solution)/shard_map/ppermute | solution.py:119
  31.7 15.8 %collective-permute-start.4 = (bf16[1168,256]{1,0:T(8,128)(2,1)S(1)}, bf16[1168,256]{1,0:T(8,128)(2,1)}, u32[]{:S(2)}, u32[]{:S(2)}) collective-permute-start(bf16[1168,256]{1,0:T(8,128)(2,1)S(1)} %collective-permute-done.refs_1_), channel_id=1, source_target_pairs={{0,4},{4,0},{1,5},{5,1},{2,6},{6,2},{3,7},{7,3},{8,12},{12,8},{9,1... | collective-permute-start | bytes 1794056 | tf_op jit(solution)/shard_map/ppermute | solution.py:119
  34.2 13.4 %collective-permute-start.5 = (bf16[1168,256]{1,0:T(8,128)(2,1)S(1)}, bf16[1168,256]{1,0:T(8,128)(2,1)}, u32[]{:S(2)}, u32[]{:S(2)}) collective-permute-start(bf16[1168,256]{1,0:T(8,128)(2,1)S(1)} %collective-permute-done.1.refs_2_), channel_id=1, source_target_pairs={{0,4},{4,0},{1,5},{5,1},{2,6},{6,2},{3,7},{7,3},{8,12},{12,8},{9,1... | collective-permute-start | bytes 1794056 | tf_op jit(solution)/shard_map/ppermute | solution.py:119
  36.1 11.5 %collective-permute-start.6 = (bf16[1168,256]{1,0:T(8,128)(2,1)S(1)}, bf16[1168,256]{1,0:T(8,128)(2,1)}, u32[]{:S(2)}, u32[]{:S(2)}) collective-permute-start(bf16[1168,256]{1,0:T(8,128)(2,1)S(1)} %collective-permute-done.2.refs_3_), channel_id=1, source_target_pairs={{0,4},{4,0},{1,5},{5,1},{2,6},{6,2},{3,7},{7,3},{8,12},{12,8},{9,1... | collective-permute-start | bytes 1794056 | tf_op jit(solution)/shard_map/ppermute | solution.py:119
  40.1 37.8 %copy-start.2 = (s32[9]{0:T(128)S(1)}, s32[9]{0:T(128)}, u32[]{:S(2)}) copy-start(s32[9]{0:T(128)} %param.9) | copy-start | bytes 112
  73.6 9.7 %all-to-all-start.2 = ((bf16[8,9,128]{2,1,0:T(8,128)(2,1)}), bf16[8,9,128]{2,1,0:T(8,128)(2,1)S(1)}, u32[]{:S(2)}, u32[]{:S(2)}) async-start(bf16[8,9,128]{2,1,0:T(8,128)(2,1)} %shard_map.57), calls=%async_computation.2 | async-start | bytes 65536 | tf_op jit(solution)/shard_map/all_to_all | solution.py:132

commit v5 on v4

--- a/solution.py
+++ b/solution.py
@@ -40,17 +40,13 @@
             values = stacked[:, pl.ds(pl.multiple_of(source * CDS, CDS), CDS)]
             labels = blocks[c * X + step][AB:].astype(F32)[:1]
             kept.append(jnp.where(row_labels == labels, values, jnp.zeros_like(values)).astype(BF))
+    kept = jnp.concatenate(kept, axis=1)
     tile = 192
     for start in range(0, AB // 2, tile):
         halves = []
         for base in (start, start + AB // 2):
-            total = None
-            for block, value in zip(blocks, kept):
-                term = lax.dot_general(
-                    block[base:base + tile], value, (((1,), (1,)), ((), ())), preferred_element_type=F32
-                )
-                total = term if total is None else total + term
-            halves.append(total)
+            part = jnp.concatenate([block[base:base + tile] for block in blocks], axis=1)
+            halves.append(lax.dot_general(part, kept, (((1,), (1,)), ((), ())), preferred_element_type=F32))
         acc[start:start + tile] = jnp.concatenate(halves, axis=1)
     pairs = CORES * OWN
     for z in range(Z):

time: 85.4 us -> 85.4 us (level)
  no operation moved by 1% of the time
where the time goes in v5:
time: 85.4 us; the launch traced here: 84.1 us
  starting transfers between devices  40.1 us (47%)
  blocking collectives  21.7 us (25%)
  waiting for transfers between devices  12.8 us (15%)
  Pallas kernels  5.72 us (7%)
  other arithmetic  2.59 us (3%)
  local copies, waits for them, and re-layouts  0.91 us (1%)
    all_to_all x1, blocking collectives, body(): partials = lax.all_to_all(partials, 'z', 0, 0, tiled=True)  21.7 us
    all_to_all x1, starting transfers between devices, body(): amps = lax.all_to_all(sent, 'z', 0, 0, tiled=True)  15.2 us
    ppermute x3, starting transfers between devices, along_x(): return lax.ppermute(value, 'x', [(i, (i + step) % X) for i in range(X)])  12 us
    ppermute x4, starting transfers between devices, body(): gathered += [lax.ppermute(value, 'core', swap) for value in gathered]  8.66 us
    all_to_all x1, waiting for transfers between devices, body(): amps = lax.all_to_all(sent, 'z', 0, 0, tiled=True)  7.44 us
    all_to_all x1, waiting for transfers between devices, body(): parts = lax.all_to_all(parts, ('x', 'core'), 0, 0, tiled=True)  5.35 us
    all_to_all x1, starting transfers between devices, body(): parts = lax.all_to_all(parts, ('x', 'core'), 0, 0, tiled=True)  4.3 us
    pallas_call x1, Pallas kernels, body(): call(multiply_kernel, shape((Z, HELD, 2 * LINE), BF), [SMEM] + [VMEM] * (...  2.99 us
  transfers between devices with their start and end apart: 9, of which 2 were waited for; matrix products, arithmetic and copies ran while one was open for 2% of the time, Pallas kernels for 1%

profile of v5, /device:TPU:24, one launch (start us, length us, event | category | flops | bytes accessed | tf_op | source)
XLA Modules:
  0.0 84.1 jit_solution(12770287047387251423)
XLA Ops:
  0.0 0.7 convert_element_type.9
  0.7 0.0 copy-start
  0.7 1.1 %pad_maximum_fusion.after.refs_0_ = bf16[1168,256]{1,0:T(8,128)(2,1)S(1)} fusion(bf16[16,256]{1,0:T(8,128)(2,1)S(1)} %broadcast_in_dim.12, bf16[1152,256]{1,0:T(8,128)(2,1)} %param.6), kind=kLoop, calls=%fused_computation | loop fusion | flops 1196032 | bytes 1196032 | tf_op jit(solution)/shard_map/concatenate | solution.py:109
  1.8 0.0 copy-start.1
  1.9 4.9 %collective-permute-start = (bf16[1168,256]{1,0:T(8,128)(2,1)S(1)}, bf16[1168,256]{1,0:T(8,128)(2,1)S(1)}, u32[]{:S(2)}, u32[]{:S(2)}) collective-permute-start(bf16[1168,256]{1,0:T(8,128)(2,1)S(1)} %pad_maximum_fusion.after.refs_0_), channel_id=1, source_target_pairs={{0,256},{128,384},{256,0},{384,128},{1,257},{129,385},{257,1},{385... | collective-permute-start | bytes 1794056 | tf_op jit(solution)/shard_map/ppermute | solution.py:100
  6.8 2.5 %collective-permute-start.1 = (bf16[1168,256]{1,0:T(8,128)(2,1)S(1)}, bf16[1168,256]{1,0:T(8,128)(2,1)S(1)}, u32[]{:S(2)}, u32[]{:S(2)}) collective-permute-start(bf16[1168,256]{1,0:T(8,128)(2,1)S(1)} %pad_maximum_fusion.after.refs_0_), channel_id=1, source_target_pairs={{0,128},{128,256},{256,384},{384,0},{1,129},{129,257},{257,385},{3... | collective-permute-start | bytes 1794056 | tf_op jit(solution)/shard_map/ppermute | solution.py:100
  9.3 4.6 %collective-permute-start.2 = (bf16[1168,256]{1,0:T(8,128)(2,1)S(1)}, bf16[1168,256]{1,0:T(8,128)(2,1)S(1)}, u32[]{:S(2)}, u32[]{:S(2)}) collective-permute-start(bf16[1168,256]{1,0:T(8,128)(2,1)S(1)} %pad_maximum_fusion.after.refs_0_), channel_id=1, source_target_pairs={{0,384},{128,0},{256,128},{384,256},{1,385},{129,1},{257,129},{385... | collective-permute-start | bytes 1794056 | tf_op jit(solution)/shard_map/ppermute | solution.py:100
  13.9 0.0 copy-done
  13.9 0.7 shard_map.55
  14.6 15.2 %all-to-all-start = ((bf16[16,4,2048]{2,1,0:T(4,128)(2,1)}), bf16[16,4,2048]{2,1,0:T(4,128)(2,1)S(1)}, u32[]{:S(2)}, u32[]{:S(2)}) async-start(bf16[16,4,2048]{2,1,0:T(4,128)(2,1)} %shard_map.55), calls=%async_computation | async-start | bytes 524288 | tf_op jit(solution)/shard_map/all_to_all | solution.py:114
  29.8 1.9 %collective-permute-start.3 = (bf16[1168,256]{1,0:T(8,128)(2,1)S(1)}, bf16[1168,256]{1,0:T(8,128)(2,1)S(1)}, u32[]{:S(2)}, u32[]{:S(2)}) collective-permute-start(bf16[1168,256]{1,0:T(8,128)(2,1)S(1)} %pad_maximum_fusion.after.refs_0_), channel_id=1, source_target_pairs={{0,4},{4,0},{1,5},{5,1},{2,6},{6,2},{3,7},{7,3},{8,12},{12,8},{9,1... | collective-permute-start | bytes 1794056 | tf_op jit(solution)/shard_map/ppermute | solution.py:115
  31.7 0.0 collective-permute-done.refs_1_
  31.7 2.4 %collective-permute-start.4 = (bf16[1168,256]{1,0:T(8,128)(2,1)S(1)}, bf16[1168,256]{1,0:T(8,128)(2,1)}, u32[]{:S(2)}, u32[]{:S(2)}) collective-permute-start(bf16[1168,256]{1,0:T(8,128)(2,1)S(1)} %collective-permute-done.refs_1_), channel_id=1, source_target_pairs={{0,4},{4,0},{1,5},{5,1},{2,6},{6,2},{3,7},{7,3},{8,12},{12,8},{9,1... | collective-permute-start | bytes 1794056 | tf_op jit(solution)/shard_map/ppermute | solution.py:115
  34.2 0.0 collective-permute-done.1.refs_2_
  34.2 1.9 %collective-permute-start.5 = (bf16[1168,256]{1,0:T(8,128)(2,1)S(1)}, bf16[1168,256]{1,0:T(8,128)(2,1)}, u32[]{:S(2)}, u32[]{:S(2)}) collective-permute-start(bf16[1168,256]{1,0:T(8,128)(2,1)S(1)} %collective-permute-done.1.refs_2_), channel_id=1, source_target_pairs={{0,4},{4,0},{1,5},{5,1},{2,6},{6,2},{3,7},{7,3},{8,12},{12,8},{9,1... | collective-permute-start | bytes 1794056 | tf_op jit(solution)/shard_map/ppermute | solution.py:115
  36.1 0.0 collective-permute-done.2.refs_3_
  36.1 2.4 %collective-permute-start.6 = (bf16[1168,256]{1,0:T(8,128)(2,1)S(1)}, bf16[1168,256]{1,0:T(8,128)(2,1)}, u32[]{:S(2)}, u32[]{:S(2)}) collective-permute-start(bf16[1168,256]{1,0:T(8,128)(2,1)S(1)} %collective-permute-done.2.refs_3_), channel_id=1, source_target_pairs={{0,4},{4,0},{1,5},{5,1},{2,6},{6,2},{3,7},{7,3},{8,12},{12,8},{9,1... | collective-permute-start | bytes 1794056 | tf_op jit(solution)/shard_map/ppermute | solution.py:115
  38.5 0.6 broadcast.7
  39.1 0.0 copy-done.1
  39.1 0.7 reduce.7
  39.8 0.1 reshape.19
  40.0 0.1 convert_element_type.12.rows
  40.0 0.1 pad_add_fusion.place
  40.1 0.0 copy-start.2
  40.1 0.0 collective-permute-done.3.refs_4_
  40.1 7.4 %all-to-all-done.amps = bf16[16,4,2048]{2,1,0:T(4,128)(2,1)S(1)} async-done(((bf16[16,4,2048]{2,1,0:T(4,128)(2,1)}), bf16[16,4,2048]{2,1,0:T(4,128)(2,1)S(1)}, u32[]{:S(2)}, u32[]{:S(2)}) %all-to-all-start) | async-done | bytes 262176 | tf_op jit(solution)/shard_map/all_to_all | solution.py:114
  47.6 0.0 collective-permute-done.4.refs_5_
  47.6 0.0 collective-permute-done.5.refs_6_
  47.6 0.0 collective-permute-done.6.refs_7_
  47.6 3.0 %shard_map.56 = bf16[16,36,128]{2,1,0:T(8,128)(2,1)S(1)} custom-call(s32[2]{0:T(128)S(1)} %pad_add_fusion.place, bf16[16,4,2048]{2,1,0:T(4,128)(2,1)S(1)} %all-to-all-done.amps, f32[64,1]{1,0:T(8,128)S(1)} %convert_element_type.12.rows, bf16[1168,256]{1,0:T(8,128)(2,1)S(1)} %pad_maximum_fusion.after.refs_0_, ...), custom_call_target="tpu_custom_call" | custom-call | tf_op jit(solution)/shard_map/pallas_call | solution.py:119
  50.6 21.7 %all_to_all.15.partials = bf16[16,36,128]{2,1,0:T(8,128)(2,1)S(1)} all-to-all(bf16[16,36,128]{2,1,0:T(8,128)(2,1)S(1)} %shard_map.56), channel_id=1, replica_groups=mesh['x'=4,'z'=16,'core'=2,'y'=4] {'z'}, dimensions={0} | all-to-all | bytes 294912 | tf_op jit(solution)/shard_map/all_to_all | solution.py:123
  72.3 1.3 %shard_map.57 = bf16[8,9,128]{2,1,0:T(8,128)(2,1)} custom-call(s32[2]{0:T(128)S(1)} %pad_add_fusion.place, bf16[16,36,128]{2,1,0:T(8,128)(2,1)S(1)} %all_to_all.15.partials), custom_call_target="tpu_custom_call" | custom-call | tf_op jit(solution)/shard_map/pallas_call | solution.py:124
  73.6 4.3 %all-to-all-start.2 = ((bf16[8,9,128]{2,1,0:T(8,128)(2,1)}), bf16[8,9,128]{2,1,0:T(8,128)(2,1)S(1)}, u32[]{:S(2)}, u32[]{:S(2)}) async-start(bf16[8,9,128]{2,1,0:T(8,128)(2,1)} %shard_map.57), calls=%async_computation.2 | async-start | bytes 65536 | tf_op jit(solution)/shard_map/all_to_all | solution.py:128
  77.9 0.0 copy-done.2
  77.9 0.1 copy.10.abs_
  78.0 5.3 %all-to-all-done.2.parts = bf16[8,9,128]{2,1,0:T(8,128)(2,1)S(1)} async-done(((bf16[8,9,128]{2,1,0:T(8,128)(2,1)}), bf16[8,9,128]{2,1,0:T(8,128)(2,1)S(1)}, u32[]{:S(2)}, u32[]{:S(2)}) %all-to-all-start.2) | async-done | bytes 18464 | tf_op jit(solution)/shard_map/all_to_all | solution.py:128
  83.4 0.7 shard_map.58
  (2 shorter events, 0.0 us)
Async XLA Ops:
  0.7 13.2 %copy-start = (bf16[1,4,32768]{2,1,0:T(4,128)(2,1)S(1)}, bf16[1,4,32768]{2,1,0:T(4,128)(2,1)}, u32[]{:S(2)}) copy-start(bf16[1,4,32768]{2,1,0:T(4,128)(2,1)} %amps.1) | copy-start | bytes 786436
  1.8 37.3 %copy-start.1 = (s32[1,512]{1,0:T(1,128)S(1)}, s32[1,512]{1,0:T(1,128)}, u32[]{:S(2)}) copy-start(s32[1,512]{1,0:T(1,128)} %rows.1) | copy-start | bytes 6148
  1.9 29.9 %collective-permute-start = (bf16[1168,256]{1,0:T(8,128)(2,1)S(1)}, bf16[1168,256]{1,0:T(8,128)(2,1)S(1)}, u32[]{:S(2)}, u32[]{:S(2)}) collective-permute-start(bf16[1168,256]{1,0:T(8,128)(2,1)S(1)} %pad_maximum_fusion.after.refs_0_), channel_id=1, source_target_pairs={{0,256},{128,384},{256,0},{384,128},{1,257},{129,385},{257,1},{385... | collective-permute-start | bytes 1794056 | tf_op jit(solution)/shard_map/ppermute | solution.py:100
  6.8 27.4 %collective-permute-start.1 = (bf16[1168,256]{1,0:T(8,128)(2,1)S(1)}, bf16[1168,256]{1,0:T(8,128)(2,1)S(1)}, u32[]{:S(2)}, u32[]{:S(2)}) collective-permute-start(bf16[1168,256]{1,0:T(8,128)(2,1)S(1)} %pad_maximum_fusion.after.refs_0_), channel_id=1, source_target_pairs={{0,128},{128,256},{256,384},{384,0},{1,129},{129,257},{257,385},{3... | collective-permute-start | bytes 1794056 | tf_op jit(solution)/shard_map/ppermute | solution.py:100
  9.3 26.8 %collective-permute-start.2 = (bf16[1168,256]{1,0:T(8,128)(2,1)S(1)}, bf16[1168,256]{1,0:T(8,128)(2,1)S(1)}, u32[]{:S(2)}, u32[]{:S(2)}) collective-permute-start(bf16[1168,256]{1,0:T(8,128)(2,1)S(1)} %pad_maximum_fusion.after.refs_0_), channel_id=1, source_target_pairs={{0,384},{128,0},{256,128},{384,256},{1,385},{129,1},{257,129},{385... | collective-permute-start | bytes 1794056 | tf_op jit(solution)/shard_map/ppermute | solution.py:100
  14.6 33.0 %all-to-all-start = ((bf16[16,4,2048]{2,1,0:T(4,128)(2,1)}), bf16[16,4,2048]{2,1,0:T(4,128)(2,1)S(1)}, u32[]{:S(2)}, u32[]{:S(2)}) async-start(bf16[16,4,2048]{2,1,0:T(4,128)(2,1)} %shard_map.55), calls=%async_computation | async-start | bytes 524288 | tf_op jit(solution)/shard_map/all_to_all | solution.py:114
  29.8 10.3 %collective-permute-start.3 = (bf16[1168,256]{1,0:T(8,128)(2,1)S(1)}, bf16[1168,256]{1,0:T(8,128)(2,1)S(1)}, u32[]{:S(2)}, u32[]{:S(2)}) collective-permute-start(bf16[1168,256]{1,0:T(8,128)(2,1)S(1)} %pad_maximum_fusion.after.refs_0_), channel_id=1, source_target_pairs={{0,4},{4,0},{1,5},{5,1},{2,6},{6,2},{3,7},{7,3},{8,12},{12,8},{9,1... | collective-permute-start | bytes 1794056 | tf_op jit(solution)/shard_map/ppermute | solution.py:115
  31.7 15.8 %collective-permute-start.4 = (bf16[1168,256]{1,0:T(8,128)(2,1)S(1)}, bf16[1168,256]{1,0:T(8,128)(2,1)}, u32[]{:S(2)}, u32[]{:S(2)}) collective-permute-start(bf16[1168,256]{1,0:T(8,128)(2,1)S(1)} %collective-permute-done.refs_1_), channel_id=1, source_target_pairs={{0,4},{4,0},{1,5},{5,1},{2,6},{6,2},{3,7},{7,3},{8,12},{12,8},{9,1... | collective-permute-start | bytes 1794056 | tf_op jit(solution)/shard_map/ppermute | solution.py:115
  34.2 13.4 %collective-permute-start.5 = (bf16[1168,256]{1,0:T(8,128)(2,1)S(1)}, bf16[1168,256]{1,0:T(8,128)(2,1)}, u32[]{:S(2)}, u32[]{:S(2)}) collective-permute-start(bf16[1168,256]{1,0:T(8,128)(2,1)S(1)} %collective-permute-done.1.refs_2_), channel_id=1, source_target_pairs={{0,4},{4,0},{1,5},{5,1},{2,6},{6,2},{3,7},{7,3},{8,12},{12,8},{9,1... | collective-permute-start | bytes 1794056 | tf_op jit(solution)/shard_map/ppermute | solution.py:115
  36.1 11.5 %collective-permute-start.6 = (bf16[1168,256]{1,0:T(8,128)(2,1)S(1)}, bf16[1168,256]{1,0:T(8,128)(2,1)}, u32[]{:S(2)}, u32[]{:S(2)}) collective-permute-start(bf16[1168,256]{1,0:T(8,128)(2,1)S(1)} %collective-permute-done.2.refs_3_), channel_id=1, source_target_pairs={{0,4},{4,0},{1,5},{5,1},{2,6},{6,2},{3,7},{7,3},{8,12},{12,8},{9,1... | collective-permute-start | bytes 1794056 | tf_op jit(solution)/shard_map/ppermute | solution.py:115
  40.1 37.8 %copy-start.2 = (s32[9]{0:T(128)S(1)}, s32[9]{0:T(128)}, u32[]{:S(2)}) copy-start(s32[9]{0:T(128)} %param.9) | copy-start | bytes 112
  73.6 9.7 %all-to-all-start.2 = ((bf16[8,9,128]{2,1,0:T(8,128)(2,1)}), bf16[8,9,128]{2,1,0:T(8,128)(2,1)S(1)}, u32[]{:S(2)}, u32[]{:S(2)}) async-start(bf16[8,9,128]{2,1,0:T(8,128)(2,1)} %shard_map.57), calls=%async_computation.2 | async-start | bytes 65536 | tf_op jit(solution)/shard_map/all_to_all | solution.py:128
